TPU v7x, 512 devices: a whole 4x8x8 slice. The times are simulated.
512 devices in a mesh: ctx: 16 (over z_lo, x, core), head: 32 (over z_hi, y).
Axes of the slice: x: 4, y: 8, z: 8 (z_hi: 4, z_lo: 2; z = z_hi * 2 + z_lo), core: 2. Of those that a mesh axis runs over, the one named last changes fastest.
Arguments:
- queries: bfloat16 [16384, 32, 128], P('ctx', 'head'), may hold values from -96 to 96
- key_states: bfloat16 [16384, 8, 128], P(('ctx', 'head')), may hold values from -4 to 4
- value_states: bfloat16 [16384, 8, 128], P(('ctx', 'head')), may hold values from -6 to 6
Outputs:
- attended: bfloat16 [16384, 32, 128], P('ctx', 'head')
All inputs are finite; a program needn't handle non-finite values.
Results may differ from a plain program's by a relative error of at most 0.0059.
Values may be sent and summed in bfloat16 or wider, within the bound.
A program may use at most 64 MiB of HBM per device.

v0:
```python
import math

import jax
import jax.numpy as jnp
from jax import lax
from jax.sharding import PartitionSpec as P


def swapped(value, axis, stride):
    mask = 2**stride
    pairs = [(source, source ^ mask) for source in range(lax.axis_size(axis))]
    return lax.ppermute(value, axis, pairs)


def from_behind(shard, axis, by):
    length = lax.axis_size(axis)
    return lax.ppermute(shard, axis, [(i, (i + by) % length) for i in range(length)])


def per_device(queries, key_states, value_states):
    cycle_size = lax.axis_size("ctx")
    row_count = queries.shape[0]
    half_rows = row_count // 2
    feature_width = queries.shape[2]
    group_size = lax.axis_size("head") // key_states.shape[1]
    score_scale = 1.0 / math.sqrt(feature_width)
    spread_keys = jnp.repeat(key_states, group_size, axis=1)
    spread_values = jnp.repeat(value_states, group_size, axis=1)
    own_keys, own_values = (
        lax.all_to_all(spread_keys, "head", split_axis=1, concat_axis=0, tiled=True),
        lax.all_to_all(spread_values, "head", split_axis=1, concat_axis=0, tiled=True),
    )
    own_keys = own_keys.reshape(row_count, feature_width)
    own_values = own_values.reshape(row_count, feature_width)
    own_index = lax.axis_index("ctx")
    partner = cycle_size - 1 - own_index
    query_rows = queries[:, 0, :]
    first_half = query_rows[:half_rows]
    moved_half = query_rows[half_rows:]
    for bit_number in range(cycle_size.bit_length() - 1):
        moved_half = swapped(moved_half, "ctx", bit_number)
    offsets = jnp.arange(half_rows, dtype=jnp.int32)
    first_pos = own_index * row_count + offsets
    moved_pos = partner * row_count + half_rows + offsets
    key_offsets = jnp.arange(row_count, dtype=jnp.int32)

    def fresh_state():
        return (
            jnp.full((half_rows,), -1e30, jnp.float32),
            jnp.zeros((half_rows,), jnp.float32),
            jnp.zeros((half_rows, feature_width), jnp.float32),
        )

    def absorb(states, block_keys, block_values, source):
        key_pos = source * row_count + key_offsets

        def update(state, query_block, query_pos):

            def compute(current):
                running_max, row_total, accumulated = current
                scores = (
                    lax.dot_general(
                        query_block,
                        block_keys,
                        (((1,), (1,)), ((), ())),
                        preferred_element_type=jnp.float32,
                    )
                    * score_scale
                )
                scores = jnp.where(key_pos[None, :] <= query_pos[:, None], scores, -1e30)
                new_max = jnp.maximum(running_max, jnp.max(scores, axis=1))
                rescale = jnp.exp(running_max - new_max)
                weights = jnp.exp(scores - new_max[:, None])
                row_total = row_total * rescale + jnp.sum(weights, axis=1)
                accumulated = accumulated * rescale[:, None] + jnp.dot(
                    weights.astype(jnp.bfloat16), block_values, preferred_element_type=jnp.float32
                )
                return (new_max, row_total, accumulated)

            needed = source * row_count <= query_pos[half_rows - 1]
            return lax.cond(needed, compute, lambda current: current, state)

        return (update(states[0], first_half, first_pos), update(states[1], moved_half, moved_pos))

    states = (fresh_state(), fresh_state())

    def turn(turn_index, carry):
        held, ahead_keys, ahead_values = carry
        held = absorb(held, ahead_keys, ahead_values, (own_index - turn_index) % cycle_size)
        ahead_keys, ahead_values = from_behind((ahead_keys, ahead_values), "ctx", 1)
        return (held, ahead_keys, ahead_values)

    states, ahead_keys, ahead_values = lax.fori_loop(
        0, cycle_size - 1, turn, (states, own_keys, own_values)
    )
    states = absorb(states, ahead_keys, ahead_values, (own_index - (cycle_size - 1)) % cycle_size)
    first_out = (states[0][2] / states[0][1][:, None]).astype(jnp.bfloat16)
    moved_out = (states[1][2] / states[1][1][:, None]).astype(jnp.bfloat16)
    for bit_number in range(cycle_size.bit_length() - 1):
        moved_out = swapped(moved_out, "ctx", bit_number)
    return jnp.concatenate([first_out, moved_out], axis=0)[:, None, :]


def solution(mesh):
    return jax.shard_map(
        per_device,
        mesh=mesh,
        in_specs=(
            P("ctx", "head", None),
            P(("ctx", "head"), None, None),
            P(("ctx", "head"), None, None),
        ),
        out_specs=P("ctx", "head", None),
        check_vma=False,
    )
```

profile of v0, /device:TPU:6, one launch (start us, length us, event | category | flops | bytes accessed | tf_op | source)
XLA Modules:
  0.0 303.9 jit_solution(404539296988998262)
XLA Ops:
  1.6 16.0 %all-to-all-start = ((bf16[32,32,128]{2,0,1:T(8,128)(2,1)}), bf16[32,32,128]{2,0,1:T(8,128)(2,1)S(1)}, u32[]{:S(2)}, u32[]{:S(2)}) async-start(bf16[32,32,128]{2,0,1:T(8,128)(2,1)} %bitcast.1), calls=%async_computation | async-start | bytes 524288 | tf_op jit(solution)/shard_map/all_to_all | solution.py:30
  18.6 1.9 collective-permute-start.2
  21.3 11.1 %all-to-all-done = bf16[32,32,128]{2,0,1:T(8,128)(2,1)S(1)} async-done(((bf16[32,32,128]{2,0,1:T(8,128)(2,1)}), bf16[32,32,128]{2,0,1:T(8,128)(2,1)S(1)}, u32[]{:S(2)}, u32[]{:S(2)}) %all-to-all-start) | async-done | bytes 262176 | tf_op jit(solution)/shard_map/all_to_all | solution.py:30
  33.2 3.9 %all-to-all-start.1 = ((bf16[32,32,128]{2,0,1:T(8,128)(2,1)}), bf16[32,32,128]{2,0,1:T(8,128)(2,1)S(1)}, u32[]{:S(2)}, u32[]{:S(2)}) async-start(bf16[32,32,128]{2,0,1:T(8,128)(2,1)} %bitcast.5), calls=%async_computation.1 | async-start | bytes 524288 | tf_op jit(solution)/shard_map/all_to_all | solution.py:31
  37.2 2.7 collective-permute-start.3
  39.9 4.1 %collective-permute-done.3 = bf16[512,128]{1,0:T(8,128)(2,1)S(1)} collective-permute-done((bf16[512,128]{1,0:T(8,128)(2,1)S(1)}, bf16[512,128]{1,0:T(8,128)(2,1)S(1)}, u32[]{:S(2)}, u32[]{:S(2)}) %collective-permute-start.3) | collective-permute-done | bytes 131104 | tf_op jit(solution)/shard_map/ppermute | solution.py:12
  44.0 3.3 %collective-permute-start.4 = (bf16[512,128]{1,0:T(8,128)(2,1)S(1)}, bf16[512,128]{1,0:T(8,128)(2,1)S(1)}, u32[]{:S(2)}, u32[]{:S(2)}) collective-permute-start(bf16[512,128]{1,0:T(8,128)(2,1)S(1)} %collective-permute-done.3), channel_id=1, source_target_pairs={{0,128},{32,160},{64,192},{96,224},{128,0},{160,32},{192,64},{224,... | collective-permute-start | bytes 393224 | tf_op jit(solution)/shard_map/ppermute | solution.py:12
  47.4 5.0 %collective-permute-done.4 = bf16[512,128]{1,0:T(8,128)(2,1)S(1)} collective-permute-done((bf16[512,128]{1,0:T(8,128)(2,1)S(1)}, bf16[512,128]{1,0:T(8,128)(2,1)S(1)}, u32[]{:S(2)}, u32[]{:S(2)}) %collective-permute-start.4) | collective-permute-done | bytes 131104 | tf_op jit(solution)/shard_map/ppermute | solution.py:12
  52.4 3.3 %collective-permute-start.5 = (bf16[512,128]{1,0:T(8,128)(2,1)S(1)}, bf16[512,128]{1,0:T(8,128)(2,1)S(1)}, u32[]{:S(2)}, u32[]{:S(2)}) collective-permute-start(bf16[512,128]{1,0:T(8,128)(2,1)S(1)} %collective-permute-done.4), channel_id=1, source_target_pairs={{0,256},{32,288},{64,320},{96,352},{128,384},{160,416},{192,448},{... | collective-permute-start | bytes 393224 | tf_op jit(solution)/shard_map/ppermute | solution.py:12
  57.0 2.3 collective-permute-done.5
  59.3 216.2 %while.30 = (s32[]{:T(128)}, f32[512]{0:T(512)S(1)}, f32[512]{0:T(512)S(1)}, f32[512,128]{1,0:T(8,128)S(1)}, f32[512]{0:T(512)S(1)}, /*index=5*/f32[512]{0:T(512...) while((s32[]{:T(128)}, f32[512]{0:T(512)S(1)}, ...), condition=%wide.region_9.10_spmd.clone, body=%wide.region_0.9_spmd.clone.sunk | while | flops 545524736 | bytes 18170528 | solution.py:93
  60.0 1.9 collective-permute-start
  62.7 3.3 %collective-permute-start.1 = (bf16[1024,128]{1,0:T(8,128)(2,1)}, bf16[1024,128]{1,0:T(8,128)(2,1)S(1)}, u32[]{:S(2)}, u32[]{:S(2)}) collective-permute-start(bf16[1024,128]{1,0:T(8,128)(2,1)} %copy.35), channel_id=1, source_target_pairs={{0,32},{32,64},{64,96},{96,128},{128,160},{160,192},{192,224},{224... | collective-permute-start | bytes 786440 | tf_op jit(solution)/shard_map/while/body/eval_jaxpr/ppermute | solution.py:17
  68.4 3.6 %conditional.10 = ((f32[512]{0:T(512)S(1)}, f32[512]{0:T(512)S(1)}, f32[512,128]{1,0:T(8,128)S(1)})) conditional(s32[]{:T(128)} %convert_element_type.62, (f32[512]{0:T(512)S(1)}, f32[512]{0:T(512)S(1)}, f32[512,128]{1,0:T(8,128)S(1)}) %tuple.89, (s32[1024]{0:T(1024)S(1)}, s32[512]{0:T(512)S(1)}, bf16[512,128]{1,0:T(8,128)(2,1)S(1)}, ...), branch_computations={%region_1.1_spmd, %region_2.4_spmd} | conditional | flops 272761856 | bytes 7510048 | solution.py:81
  72.0 3.6 %conditional.11 = ((f32[512]{0:T(512)S(1)}, f32[512]{0:T(512)S(1)}, f32[512,128]{1,0:T(8,128)S(1)})) conditional(s32[]{:T(128)} %convert_element_type.63, (f32[512]{0:T(512)S(1)}, f32[512]{0:T(512)S(1)}, f32[512,128]{1,0:T(8,128)S(1)}) %tuple.91, (s32[1024]{0:T(1024)S(1)}, s32[512]{0:T(512)S(1)}, bf16[512,128]{1,0:T(8,128)(2,1)S(1)}, ...), branch_computations={%region_5.5_spmd, %region_6.8_spmd} | conditional | flops 272761856 | bytes 7510048 | solution.py:81
  76.4 1.9 collective-permute-start
  79.0 1.9 collective-permute-start.1
  83.4 3.6 %conditional.10 = ((f32[512]{0:T(512)S(1)}, f32[512]{0:T(512)S(1)}, f32[512,128]{1,0:T(8,128)S(1)})) conditional(s32[]{:T(128)} %convert_element_type.62, (f32[512]{0:T(512)S(1)}, f32[512]{0:T(512)S(1)}, f32[512,128]{1,0:T(8,128)S(1)}) %tuple.89, (s32[1024]{0:T(1024)S(1)}, s32[512]{0:T(512)S(1)}, bf16[512,128]{1,0:T(8,128)(2,1)S(1)}, ...), branch_computations={%region_1.1_spmd, %region_2.4_spmd} | conditional | flops 272761856 | bytes 7510048 | solution.py:81
  87.0 3.6 %conditional.11 = ((f32[512]{0:T(512)S(1)}, f32[512]{0:T(512)S(1)}, f32[512,128]{1,0:T(8,128)S(1)})) conditional(s32[]{:T(128)} %convert_element_type.63, (f32[512]{0:T(512)S(1)}, f32[512]{0:T(512)S(1)}, f32[512,128]{1,0:T(8,128)S(1)}) %tuple.91, (s32[1024]{0:T(1024)S(1)}, s32[512]{0:T(512)S(1)}, bf16[512,128]{1,0:T(8,128)(2,1)S(1)}, ...), branch_computations={%region_5.5_spmd, %region_6.8_spmd} | conditional | flops 272761856 | bytes 7510048 | solution.py:81
  91.3 1.9 collective-permute-start
  93.9 1.9 collective-permute-start.1
  98.3 3.6 %conditional.10 = ((f32[512]{0:T(512)S(1)}, f32[512]{0:T(512)S(1)}, f32[512,128]{1,0:T(8,128)S(1)})) conditional(s32[]{:T(128)} %convert_element_type.62, (f32[512]{0:T(512)S(1)}, f32[512]{0:T(512)S(1)}, f32[512,128]{1,0:T(8,128)S(1)}) %tuple.89, (s32[1024]{0:T(1024)S(1)}, s32[512]{0:T(512)S(1)}, bf16[512,128]{1,0:T(8,128)(2,1)S(1)}, ...), branch_computations={%region_1.1_spmd, %region_2.4_spmd} | conditional | flops 272761856 | bytes 7510048 | solution.py:81
  101.9 3.6 %conditional.11 = ((f32[512]{0:T(512)S(1)}, f32[512]{0:T(512)S(1)}, f32[512,128]{1,0:T(8,128)S(1)})) conditional(s32[]{:T(128)} %convert_element_type.63, (f32[512]{0:T(512)S(1)}, f32[512]{0:T(512)S(1)}, f32[512,128]{1,0:T(8,128)S(1)}) %tuple.91, (s32[1024]{0:T(1024)S(1)}, s32[512]{0:T(512)S(1)}, bf16[512,128]{1,0:T(8,128)(2,1)S(1)}, ...), branch_computations={%region_5.5_spmd, %region_6.8_spmd} | conditional | flops 272761856 | bytes 7510048 | solution.py:81
  106.2 1.9 collective-permute-start
  108.9 1.9 collective-permute-start.1
  113.2 3.6 %conditional.10 = ((f32[512]{0:T(512)S(1)}, f32[512]{0:T(512)S(1)}, f32[512,128]{1,0:T(8,128)S(1)})) conditional(s32[]{:T(128)} %convert_element_type.62, (f32[512]{0:T(512)S(1)}, f32[512]{0:T(512)S(1)}, f32[512,128]{1,0:T(8,128)S(1)}) %tuple.89, (s32[1024]{0:T(1024)S(1)}, s32[512]{0:T(512)S(1)}, bf16[512,128]{1,0:T(8,128)(2,1)S(1)}, ...), branch_computations={%region_1.1_spmd, %region_2.4_spmd} | conditional | flops 272761856 | bytes 7510048 | solution.py:81
  116.8 3.6 %conditional.11 = ((f32[512]{0:T(512)S(1)}, f32[512]{0:T(512)S(1)}, f32[512,128]{1,0:T(8,128)S(1)})) conditional(s32[]{:T(128)} %convert_element_type.63, (f32[512]{0:T(512)S(1)}, f32[512]{0:T(512)S(1)}, f32[512,128]{1,0:T(8,128)S(1)}) %tuple.91, (s32[1024]{0:T(1024)S(1)}, s32[512]{0:T(512)S(1)}, bf16[512,128]{1,0:T(8,128)(2,1)S(1)}, ...), branch_computations={%region_5.5_spmd, %region_6.8_spmd} | conditional | flops 272761856 | bytes 7510048 | solution.py:81
  121.2 1.9 collective-permute-start
  123.8 1.9 collective-permute-start.1
  128.2 3.6 %conditional.10 = ((f32[512]{0:T(512)S(1)}, f32[512]{0:T(512)S(1)}, f32[512,128]{1,0:T(8,128)S(1)})) conditional(s32[]{:T(128)} %convert_element_type.62, (f32[512]{0:T(512)S(1)}, f32[512]{0:T(512)S(1)}, f32[512,128]{1,0:T(8,128)S(1)}) %tuple.89, (s32[1024]{0:T(1024)S(1)}, s32[512]{0:T(512)S(1)}, bf16[512,128]{1,0:T(8,128)(2,1)S(1)}, ...), branch_computations={%region_1.1_spmd, %region_2.4_spmd} | conditional | flops 272761856 | bytes 7510048 | solution.py:81
  131.8 3.6 %conditional.11 = ((f32[512]{0:T(512)S(1)}, f32[512]{0:T(512)S(1)}, f32[512,128]{1,0:T(8,128)S(1)})) conditional(s32[]{:T(128)} %convert_element_type.63, (f32[512]{0:T(512)S(1)}, f32[512]{0:T(512)S(1)}, f32[512,128]{1,0:T(8,128)S(1)}) %tuple.91, (s32[1024]{0:T(1024)S(1)}, s32[512]{0:T(512)S(1)}, bf16[512,128]{1,0:T(8,128)(2,1)S(1)}, ...), branch_computations={%region_5.5_spmd, %region_6.8_spmd} | conditional | flops 272761856 | bytes 7510048 | solution.py:81
  136.1 1.9 collective-permute-start
  138.7 1.9 collective-permute-start.1
  143.1 3.6 %conditional.10 = ((f32[512]{0:T(512)S(1)}, f32[512]{0:T(512)S(1)}, f32[512,128]{1,0:T(8,128)S(1)})) conditional(s32[]{:T(128)} %convert_element_type.62, (f32[512]{0:T(512)S(1)}, f32[512]{0:T(512)S(1)}, f32[512,128]{1,0:T(8,128)S(1)}) %tuple.89, (s32[1024]{0:T(1024)S(1)}, s32[512]{0:T(512)S(1)}, bf16[512,128]{1,0:T(8,128)(2,1)S(1)}, ...), branch_computations={%region_1.1_spmd, %region_2.4_spmd} | conditional | flops 272761856 | bytes 7510048 | solution.py:81
  146.7 3.6 %conditional.11 = ((f32[512]{0:T(512)S(1)}, f32[512]{0:T(512)S(1)}, f32[512,128]{1,0:T(8,128)S(1)})) conditional(s32[]{:T(128)} %convert_element_type.63, (f32[512]{0:T(512)S(1)}, f32[512]{0:T(512)S(1)}, f32[512,128]{1,0:T(8,128)S(1)}) %tuple.91, (s32[1024]{0:T(1024)S(1)}, s32[512]{0:T(512)S(1)}, bf16[512,128]{1,0:T(8,128)(2,1)S(1)}, ...), branch_computations={%region_5.5_spmd, %region_6.8_spmd} | conditional | flops 272761856 | bytes 7510048 | solution.py:81
  151.1 1.9 collective-permute-start
  153.7 1.9 collective-permute-start.1
  158.1 3.6 %conditional.10 = ((f32[512]{0:T(512)S(1)}, f32[512]{0:T(512)S(1)}, f32[512,128]{1,0:T(8,128)S(1)})) conditional(s32[]{:T(128)} %convert_element_type.62, (f32[512]{0:T(512)S(1)}, f32[512]{0:T(512)S(1)}, f32[512,128]{1,0:T(8,128)S(1)}) %tuple.89, (s32[1024]{0:T(1024)S(1)}, s32[512]{0:T(512)S(1)}, bf16[512,128]{1,0:T(8,128)(2,1)S(1)}, ...), branch_computations={%region_1.1_spmd, %region_2.4_spmd} | conditional | flops 272761856 | bytes 7510048 | solution.py:81
  161.7 3.6 %conditional.11 = ((f32[512]{0:T(512)S(1)}, f32[512]{0:T(512)S(1)}, f32[512,128]{1,0:T(8,128)S(1)})) conditional(s32[]{:T(128)} %convert_element_type.63, (f32[512]{0:T(512)S(1)}, f32[512]{0:T(512)S(1)}, f32[512,128]{1,0:T(8,128)S(1)}) %tuple.91, (s32[1024]{0:T(1024)S(1)}, s32[512]{0:T(512)S(1)}, bf16[512,128]{1,0:T(8,128)(2,1)S(1)}, ...), branch_computations={%region_5.5_spmd, %region_6.8_spmd} | conditional | flops 272761856 | bytes 7510048 | solution.py:81
  173.9 2.8 collective-permute-done.1
  177.4 5.4 %collective-permute-start = (bf16[1024,128]{1,0:T(8,128)(2,1)}, bf16[1024,128]{1,0:T(8,128)(2,1)S(1)}, u32[]{:S(2)}, u32[]{:S(2)}) collective-permute-start(bf16[1024,128]{1,0:T(8,128)(2,1)} %copy.34), channel_id=1, source_target_pairs={{0,32},{32,64},{64,96},{96,128},{128,160},{160,192},{192,224},{224... | collective-permute-start | bytes 786440 | tf_op jit(solution)/shard_map/while/body/eval_jaxpr/ppermute | solution.py:17
  183.5 2.1 collective-permute-start.1
  188.2 3.2 %collective-permute-done.1 = bf16[1024,128]{1,0:T(8,128)(2,1)S(1)} collective-permute-done((bf16[1024,128]{1,0:T(8,128)(2,1)}, bf16[1024,128]{1,0:T(8,128)(2,1)S(1)}, u32[]{:S(2)}, u32[]{:S(2)}) %collective-permute-start.1) | collective-permute-done | bytes 262176 | tf_op jit(solution)/shard_map/while/body/eval_jaxpr/ppermute | solution.py:17
  192.1 1.9 collective-permute-start
  194.7 5.8 %collective-permute-start.1 = (bf16[1024,128]{1,0:T(8,128)(2,1)}, bf16[1024,128]{1,0:T(8,128)(2,1)S(1)}, u32[]{:S(2)}, u32[]{:S(2)}) collective-permute-start(bf16[1024,128]{1,0:T(8,128)(2,1)} %copy.35), channel_id=1, source_target_pairs={{0,32},{32,64},{64,96},{96,128},{128,160},{160,192},{192,224},{224... | collective-permute-start | bytes 786440 | tf_op jit(solution)/shard_map/while/body/eval_jaxpr/ppermute | solution.py:17
  203.9 3.1 %collective-permute-start = (bf16[1024,128]{1,0:T(8,128)(2,1)}, bf16[1024,128]{1,0:T(8,128)(2,1)S(1)}, u32[]{:S(2)}, u32[]{:S(2)}) collective-permute-start(bf16[1024,128]{1,0:T(8,128)(2,1)} %copy.34), channel_id=1, source_target_pairs={{0,32},{32,64},{64,96},{96,128},{128,160},{160,192},{192,224},{224... | collective-permute-start | bytes 786440 | tf_op jit(solution)/shard_map/while/body/eval_jaxpr/ppermute | solution.py:17
  207.7 6.4 %collective-permute-start.1 = (bf16[1024,128]{1,0:T(8,128)(2,1)}, bf16[1024,128]{1,0:T(8,128)(2,1)S(1)}, u32[]{:S(2)}, u32[]{:S(2)}) collective-permute-start(bf16[1024,128]{1,0:T(8,128)(2,1)} %copy.35), channel_id=1, source_target_pairs={{0,32},{32,64},{64,96},{96,128},{128,160},{160,192},{192,224},{224... | collective-permute-start | bytes 786440 | tf_op jit(solution)/shard_map/while/body/eval_jaxpr/ppermute | solution.py:17
  217.4 4.4 %collective-permute-start = (bf16[1024,128]{1,0:T(8,128)(2,1)}, bf16[1024,128]{1,0:T(8,128)(2,1)S(1)}, u32[]{:S(2)}, u32[]{:S(2)}) collective-permute-start(bf16[1024,128]{1,0:T(8,128)(2,1)} %copy.34), channel_id=1, source_target_pairs={{0,32},{32,64},{64,96},{96,128},{128,160},{160,192},{192,224},{224... | collective-permute-start | bytes 786440 | tf_op jit(solution)/shard_map/while/body/eval_jaxpr/ppermute | solution.py:17
  222.5 6.4 %collective-permute-start.1 = (bf16[1024,128]{1,0:T(8,128)(2,1)}, bf16[1024,128]{1,0:T(8,128)(2,1)S(1)}, u32[]{:S(2)}, u32[]{:S(2)}) collective-permute-start(bf16[1024,128]{1,0:T(8,128)(2,1)} %copy.35), channel_id=1, source_target_pairs={{0,32},{32,64},{64,96},{96,128},{128,160},{160,192},{192,224},{224... | collective-permute-start | bytes 786440 | tf_op jit(solution)/shard_map/while/body/eval_jaxpr/ppermute | solution.py:17
  232.1 3.1 %collective-permute-start = (bf16[1024,128]{1,0:T(8,128)(2,1)}, bf16[1024,128]{1,0:T(8,128)(2,1)S(1)}, u32[]{:S(2)}, u32[]{:S(2)}) collective-permute-start(bf16[1024,128]{1,0:T(8,128)(2,1)} %copy.34), channel_id=1, source_target_pairs={{0,32},{32,64},{64,96},{96,128},{128,160},{160,192},{192,224},{224... | collective-permute-start | bytes 786440 | tf_op jit(solution)/shard_map/while/body/eval_jaxpr/ppermute | solution.py:17
  236.0 6.4 %collective-permute-start.1 = (bf16[1024,128]{1,0:T(8,128)(2,1)}, bf16[1024,128]{1,0:T(8,128)(2,1)S(1)}, u32[]{:S(2)}, u32[]{:S(2)}) collective-permute-start(bf16[1024,128]{1,0:T(8,128)(2,1)} %copy.35), channel_id=1, source_target_pairs={{0,32},{32,64},{64,96},{96,128},{128,160},{160,192},{192,224},{224... | collective-permute-start | bytes 786440 | tf_op jit(solution)/shard_map/while/body/eval_jaxpr/ppermute | solution.py:17
  245.6 3.1 %collective-permute-start = (bf16[1024,128]{1,0:T(8,128)(2,1)}, bf16[1024,128]{1,0:T(8,128)(2,1)S(1)}, u32[]{:S(2)}, u32[]{:S(2)}) collective-permute-start(bf16[1024,128]{1,0:T(8,128)(2,1)} %copy.34), channel_id=1, source_target_pairs={{0,32},{32,64},{64,96},{96,128},{128,160},{160,192},{192,224},{224... | collective-permute-start | bytes 786440 | tf_op jit(solution)/shard_map/while/body/eval_jaxpr/ppermute | solution.py:17
  249.5 6.4 %collective-permute-start.1 = (bf16[1024,128]{1,0:T(8,128)(2,1)}, bf16[1024,128]{1,0:T(8,128)(2,1)S(1)}, u32[]{:S(2)}, u32[]{:S(2)}) collective-permute-start(bf16[1024,128]{1,0:T(8,128)(2,1)} %copy.35), channel_id=1, source_target_pairs={{0,32},{32,64},{64,96},{96,128},{128,160},{160,192},{192,224},{224... | collective-permute-start | bytes 786440 | tf_op jit(solution)/shard_map/while/body/eval_jaxpr/ppermute | solution.py:17
  258.4 3.6 %conditional.11 = ((f32[512]{0:T(512)S(1)}, f32[512]{0:T(512)S(1)}, f32[512,128]{1,0:T(8,128)S(1)})) conditional(s32[]{:T(128)} %convert_element_type.63, (f32[512]{0:T(512)S(1)}, f32[512]{0:T(512)S(1)}, f32[512,128]{1,0:T(8,128)S(1)}) %tuple.91, (s32[1024]{0:T(1024)S(1)}, s32[512]{0:T(512)S(1)}, bf16[512,128]{1,0:T(8,128)(2,1)S(1)}, ...), branch_computations={%region_5.5_spmd, %region_6.8_spmd} | conditional | flops 272761856 | bytes 7510048 | solution.py:81
  262.7 1.9 collective-permute-start
  265.3 4.1 %collective-permute-start.1 = (bf16[1024,128]{1,0:T(8,128)(2,1)}, bf16[1024,128]{1,0:T(8,128)(2,1)S(1)}, u32[]{:S(2)}, u32[]{:S(2)}) collective-permute-start(bf16[1024,128]{1,0:T(8,128)(2,1)} %copy.35), channel_id=1, source_target_pairs={{0,32},{32,64},{64,96},{96,128},{128,160},{160,192},{192,224},{224... | collective-permute-start | bytes 786440 | tf_op jit(solution)/shard_map/while/body/eval_jaxpr/ppermute | solution.py:17
  271.9 3.6 %conditional.11 = ((f32[512]{0:T(512)S(1)}, f32[512]{0:T(512)S(1)}, f32[512,128]{1,0:T(8,128)S(1)})) conditional(s32[]{:T(128)} %convert_element_type.63, (f32[512]{0:T(512)S(1)}, f32[512]{0:T(512)S(1)}, f32[512,128]{1,0:T(8,128)S(1)}) %tuple.91, (s32[1024]{0:T(1024)S(1)}, s32[512]{0:T(512)S(1)}, bf16[512,128]{1,0:T(8,128)(2,1)S(1)}, ...), branch_computations={%region_5.5_spmd, %region_6.8_spmd} | conditional | flops 272761856 | bytes 7510048 | solution.py:81
  277.3 1.9 collective-permute-start.6
  280.6 1.9 collective-permute-start.7
  282.5 5.5 %collective-permute-done.7 = bf16[512,128]{1,0:T(8,128)(2,1)S(1)} collective-permute-done((bf16[512,128]{1,0:T(8,128)(2,1)S(1)}, bf16[512,128]{1,0:T(8,128)(2,1)S(1)}, u32[]{:S(2)}, u32[]{:S(2)}) %collective-permute-start.7) | collective-permute-done | bytes 131104 | tf_op jit(solution)/shard_map/ppermute | solution.py:12
  288.0 1.9 collective-permute-start.8
  291.2 5.2 %collective-permute-done.8 = bf16[512,128]{1,0:T(8,128)(2,1)S(1)} collective-permute-done((bf16[512,128]{1,0:T(8,128)(2,1)S(1)}, bf16[512,128]{1,0:T(8,128)(2,1)S(1)}, u32[]{:S(2)}, u32[]{:S(2)}) %collective-permute-start.8) | collective-permute-done | bytes 131104 | tf_op jit(solution)/shard_map/ppermute | solution.py:12
  296.4 1.9 collective-permute-start.9
  298.4 4.8 %collective-permute-done.9 = bf16[512,128]{1,0:T(8,128)(2,1)S(1)} collective-permute-done((bf16[512,128]{1,0:T(8,128)(2,1)S(1)}, bf16[512,128]{1,0:T(8,128)(2,1)S(1)}, u32[]{:S(2)}, u32[]{:S(2)}) %collective-permute-start.9) | collective-permute-done | bytes 131104 | tf_op jit(solution)/shard_map/ppermute | solution.py:12
  (243 shorter events, 112.4 us)
Async XLA Ops:
  1.6 30.9 %all-to-all-start = ((bf16[32,32,128]{2,0,1:T(8,128)(2,1)}), bf16[32,32,128]{2,0,1:T(8,128)(2,1)S(1)}, u32[]{:S(2)}, u32[]{:S(2)}) async-start(bf16[32,32,128]{2,0,1:T(8,128)(2,1)} %bitcast.1), calls=%async_computation | async-start | bytes 524288 | tf_op jit(solution)/shard_map/all_to_all | solution.py:30
  18.6 18.6 %collective-permute-start.2 = (bf16[512,128]{1,0:T(8,128)(2,1)S(1)}, bf16[512,128]{1,0:T(8,128)(2,1)S(1)}, u32[]{:S(2)}, u32[]{:S(2)}) collective-permute-start(bf16[512,128]{1,0:T(8,128)(2,1)S(1)} %get-tuple-element.613), channel_id=1, source_target_pairs={{0,32},{32,0},{64,96},{96,64},{128,160},{160,128},{192,224},{224,1... | collective-permute-start | bytes 393224 | tf_op jit(solution)/shard_map/ppermute | solution.py:12
  33.2 23.7 %all-to-all-start.1 = ((bf16[32,32,128]{2,0,1:T(8,128)(2,1)}), bf16[32,32,128]{2,0,1:T(8,128)(2,1)S(1)}, u32[]{:S(2)}, u32[]{:S(2)}) async-start(bf16[32,32,128]{2,0,1:T(8,128)(2,1)} %bitcast.5), calls=%async_computation.1 | async-start | bytes 524288 | tf_op jit(solution)/shard_map/all_to_all | solution.py:31
  37.2 6.9 %collective-permute-start.3 = (bf16[512,128]{1,0:T(8,128)(2,1)S(1)}, bf16[512,128]{1,0:T(8,128)(2,1)S(1)}, u32[]{:S(2)}, u32[]{:S(2)}) collective-permute-start(bf16[512,128]{1,0:T(8,128)(2,1)S(1)} %collective-permute-done.2), channel_id=1, source_target_pairs={{0,64},{32,96},{64,0},{96,32},{128,192},{160,224},{192,128},{224,1... | collective-permute-start | bytes 393224 | tf_op jit(solution)/shard_map/ppermute | solution.py:12
  44.0 8.4 %collective-permute-start.4 = (bf16[512,128]{1,0:T(8,128)(2,1)S(1)}, bf16[512,128]{1,0:T(8,128)(2,1)S(1)}, u32[]{:S(2)}, u32[]{:S(2)}) collective-permute-start(bf16[512,128]{1,0:T(8,128)(2,1)S(1)} %collective-permute-done.3), channel_id=1, source_target_pairs={{0,128},{32,160},{64,192},{96,224},{128,0},{160,32},{192,64},{224,... | collective-permute-start | bytes 393224 | tf_op jit(solution)/shard_map/ppermute | solution.py:12
  52.4 6.8 %collective-permute-start.5 = (bf16[512,128]{1,0:T(8,128)(2,1)S(1)}, bf16[512,128]{1,0:T(8,128)(2,1)S(1)}, u32[]{:S(2)}, u32[]{:S(2)}) collective-permute-start(bf16[512,128]{1,0:T(8,128)(2,1)S(1)} %collective-permute-done.4), channel_id=1, source_target_pairs={{0,256},{32,288},{64,320},{96,352},{128,384},{160,416},{192,448},{... | collective-permute-start | bytes 393224 | tf_op jit(solution)/shard_map/ppermute | solution.py:12
  60.0 15.6 %collective-permute-start = (bf16[1024,128]{1,0:T(8,128)(2,1)}, bf16[1024,128]{1,0:T(8,128)(2,1)S(1)}, u32[]{:S(2)}, u32[]{:S(2)}) collective-permute-start(bf16[1024,128]{1,0:T(8,128)(2,1)} %copy.34), channel_id=1, source_target_pairs={{0,32},{32,64},{64,96},{96,128},{128,160},{160,192},{192,224},{224... | collective-permute-start | bytes 786440 | tf_op jit(solution)/shard_map/while/body/eval_jaxpr/ppermute | solution.py:17
  62.7 13.0 %collective-permute-start.1 = (bf16[1024,128]{1,0:T(8,128)(2,1)}, bf16[1024,128]{1,0:T(8,128)(2,1)S(1)}, u32[]{:S(2)}, u32[]{:S(2)}) collective-permute-start(bf16[1024,128]{1,0:T(8,128)(2,1)} %copy.35), channel_id=1, source_target_pairs={{0,32},{32,64},{64,96},{96,128},{128,160},{160,192},{192,224},{224... | collective-permute-start | bytes 786440 | tf_op jit(solution)/shard_map/while/body/eval_jaxpr/ppermute | solution.py:17
  76.4 14.2 %collective-permute-start = (bf16[1024,128]{1,0:T(8,128)(2,1)}, bf16[1024,128]{1,0:T(8,128)(2,1)S(1)}, u32[]{:S(2)}, u32[]{:S(2)}) collective-permute-start(bf16[1024,128]{1,0:T(8,128)(2,1)} %copy.34), channel_id=1, source_target_pairs={{0,32},{32,64},{64,96},{96,128},{128,160},{160,192},{192,224},{224... | collective-permute-start | bytes 786440 | tf_op jit(solution)/shard_map/while/body/eval_jaxpr/ppermute | solution.py:17
  79.0 11.6 %collective-permute-start.1 = (bf16[1024,128]{1,0:T(8,128)(2,1)}, bf16[1024,128]{1,0:T(8,128)(2,1)S(1)}, u32[]{:S(2)}, u32[]{:S(2)}) collective-permute-start(bf16[1024,128]{1,0:T(8,128)(2,1)} %copy.35), channel_id=1, source_target_pairs={{0,32},{32,64},{64,96},{96,128},{128,160},{160,192},{192,224},{224... | collective-permute-start | bytes 786440 | tf_op jit(solution)/shard_map/while/body/eval_jaxpr/ppermute | solution.py:17
  91.3 14.2 %collective-permute-start = (bf16[1024,128]{1,0:T(8,128)(2,1)}, bf16[1024,128]{1,0:T(8,128)(2,1)S(1)}, u32[]{:S(2)}, u32[]{:S(2)}) collective-permute-start(bf16[1024,128]{1,0:T(8,128)(2,1)} %copy.34), channel_id=1, source_target_pairs={{0,32},{32,64},{64,96},{96,128},{128,160},{160,192},{192,224},{224... | collective-permute-start | bytes 786440 | tf_op jit(solution)/shard_map/while/body/eval_jaxpr/ppermute | solution.py:17
  93.9 11.6 %collective-permute-start.1 = (bf16[1024,128]{1,0:T(8,128)(2,1)}, bf16[1024,128]{1,0:T(8,128)(2,1)S(1)}, u32[]{:S(2)}, u32[]{:S(2)}) collective-permute-start(bf16[1024,128]{1,0:T(8,128)(2,1)} %copy.35), channel_id=1, source_target_pairs={{0,32},{32,64},{64,96},{96,128},{128,160},{160,192},{192,224},{224... | collective-permute-start | bytes 786440 | tf_op jit(solution)/shard_map/while/body/eval_jaxpr/ppermute | solution.py:17
  106.2 14.2 %collective-permute-start = (bf16[1024,128]{1,0:T(8,128)(2,1)}, bf16[1024,128]{1,0:T(8,128)(2,1)S(1)}, u32[]{:S(2)}, u32[]{:S(2)}) collective-permute-start(bf16[1024,128]{1,0:T(8,128)(2,1)} %copy.34), channel_id=1, source_target_pairs={{0,32},{32,64},{64,96},{96,128},{128,160},{160,192},{192,224},{224... | collective-permute-start | bytes 786440 | tf_op jit(solution)/shard_map/while/body/eval_jaxpr/ppermute | solution.py:17
  108.9 11.6 %collective-permute-start.1 = (bf16[1024,128]{1,0:T(8,128)(2,1)}, bf16[1024,128]{1,0:T(8,128)(2,1)S(1)}, u32[]{:S(2)}, u32[]{:S(2)}) collective-permute-start(bf16[1024,128]{1,0:T(8,128)(2,1)} %copy.35), channel_id=1, source_target_pairs={{0,32},{32,64},{64,96},{96,128},{128,160},{160,192},{192,224},{224... | collective-permute-start | bytes 786440 | tf_op jit(solution)/shard_map/while/body/eval_jaxpr/ppermute | solution.py:17
  121.2 14.2 %collective-permute-start = (bf16[1024,128]{1,0:T(8,128)(2,1)}, bf16[1024,128]{1,0:T(8,128)(2,1)S(1)}, u32[]{:S(2)}, u32[]{:S(2)}) collective-permute-start(bf16[1024,128]{1,0:T(8,128)(2,1)} %copy.34), channel_id=1, source_target_pairs={{0,32},{32,64},{64,96},{96,128},{128,160},{160,192},{192,224},{224... | collective-permute-start | bytes 786440 | tf_op jit(solution)/shard_map/while/body/eval_jaxpr/ppermute | solution.py:17
  123.8 11.6 %collective-permute-start.1 = (bf16[1024,128]{1,0:T(8,128)(2,1)}, bf16[1024,128]{1,0:T(8,128)(2,1)S(1)}, u32[]{:S(2)}, u32[]{:S(2)}) collective-permute-start(bf16[1024,128]{1,0:T(8,128)(2,1)} %copy.35), channel_id=1, source_target_pairs={{0,32},{32,64},{64,96},{96,128},{128,160},{160,192},{192,224},{224... | collective-permute-start | bytes 786440 | tf_op jit(solution)/shard_map/while/body/eval_jaxpr/ppermute | solution.py:17
  136.1 14.2 %collective-permute-start = (bf16[1024,128]{1,0:T(8,128)(2,1)}, bf16[1024,128]{1,0:T(8,128)(2,1)S(1)}, u32[]{:S(2)}, u32[]{:S(2)}) collective-permute-start(bf16[1024,128]{1,0:T(8,128)(2,1)} %copy.34), channel_id=1, source_target_pairs={{0,32},{32,64},{64,96},{96,128},{128,160},{160,192},{192,224},{224... | collective-permute-start | bytes 786440 | tf_op jit(solution)/shard_map/while/body/eval_jaxpr/ppermute | solution.py:17
  138.7 11.6 %collective-permute-start.1 = (bf16[1024,128]{1,0:T(8,128)(2,1)}, bf16[1024,128]{1,0:T(8,128)(2,1)S(1)}, u32[]{:S(2)}, u32[]{:S(2)}) collective-permute-start(bf16[1024,128]{1,0:T(8,128)(2,1)} %copy.35), channel_id=1, source_target_pairs={{0,32},{32,64},{64,96},{96,128},{128,160},{160,192},{192,224},{224... | collective-permute-start | bytes 786440 | tf_op jit(solution)/shard_map/while/body/eval_jaxpr/ppermute | solution.py:17
  151.1 14.2 %collective-permute-start = (bf16[1024,128]{1,0:T(8,128)(2,1)}, bf16[1024,128]{1,0:T(8,128)(2,1)S(1)}, u32[]{:S(2)}, u32[]{:S(2)}) collective-permute-start(bf16[1024,128]{1,0:T(8,128)(2,1)} %copy.34), channel_id=1, source_target_pairs={{0,32},{32,64},{64,96},{96,128},{128,160},{160,192},{192,224},{224... | collective-permute-start | bytes 786440 | tf_op jit(solution)/shard_map/while/body/eval_jaxpr/ppermute | solution.py:17
  153.7 11.6 %collective-permute-start.1 = (bf16[1024,128]{1,0:T(8,128)(2,1)}, bf16[1024,128]{1,0:T(8,128)(2,1)S(1)}, u32[]{:S(2)}, u32[]{:S(2)}) collective-permute-start(bf16[1024,128]{1,0:T(8,128)(2,1)} %copy.35), channel_id=1, source_target_pairs={{0,32},{32,64},{64,96},{96,128},{128,160},{160,192},{192,224},{224... | collective-permute-start | bytes 786440 | tf_op jit(solution)/shard_map/while/body/eval_jaxpr/ppermute | solution.py:17
  166.0 7.9 %collective-permute-start = (bf16[1024,128]{1,0:T(8,128)(2,1)}, bf16[1024,128]{1,0:T(8,128)(2,1)S(1)}, u32[]{:S(2)}, u32[]{:S(2)}) collective-permute-start(bf16[1024,128]{1,0:T(8,128)(2,1)} %copy.34), channel_id=1, source_target_pairs={{0,32},{32,64},{64,96},{96,128},{128,160},{160,192},{192,224},{224... | collective-permute-start | bytes 786440 | tf_op jit(solution)/shard_map/while/body/eval_jaxpr/ppermute | solution.py:17
  168.6 8.1 %collective-permute-start.1 = (bf16[1024,128]{1,0:T(8,128)(2,1)}, bf16[1024,128]{1,0:T(8,128)(2,1)S(1)}, u32[]{:S(2)}, u32[]{:S(2)}) collective-permute-start(bf16[1024,128]{1,0:T(8,128)(2,1)} %copy.35), channel_id=1, source_target_pairs={{0,32},{32,64},{64,96},{96,128},{128,160},{160,192},{192,224},{224... | collective-permute-start | bytes 786440 | tf_op jit(solution)/shard_map/while/body/eval_jaxpr/ppermute | solution.py:17
  177.4 10.8 %collective-permute-start = (bf16[1024,128]{1,0:T(8,128)(2,1)}, bf16[1024,128]{1,0:T(8,128)(2,1)S(1)}, u32[]{:S(2)}, u32[]{:S(2)}) collective-permute-start(bf16[1024,128]{1,0:T(8,128)(2,1)} %copy.34), channel_id=1, source_target_pairs={{0,32},{32,64},{64,96},{96,128},{128,160},{160,192},{192,224},{224... | collective-permute-start | bytes 786440 | tf_op jit(solution)/shard_map/while/body/eval_jaxpr/ppermute | solution.py:17
  183.5 7.9 %collective-permute-start.1 = (bf16[1024,128]{1,0:T(8,128)(2,1)}, bf16[1024,128]{1,0:T(8,128)(2,1)S(1)}, u32[]{:S(2)}, u32[]{:S(2)}) collective-permute-start(bf16[1024,128]{1,0:T(8,128)(2,1)} %copy.35), channel_id=1, source_target_pairs={{0,32},{32,64},{64,96},{96,128},{128,160},{160,192},{192,224},{224... | collective-permute-start | bytes 786440 | tf_op jit(solution)/shard_map/while/body/eval_jaxpr/ppermute | solution.py:17
  192.1 11.0 %collective-permute-start = (bf16[1024,128]{1,0:T(8,128)(2,1)}, bf16[1024,128]{1,0:T(8,128)(2,1)S(1)}, u32[]{:S(2)}, u32[]{:S(2)}) collective-permute-start(bf16[1024,128]{1,0:T(8,128)(2,1)} %copy.34), channel_id=1, source_target_pairs={{0,32},{32,64},{64,96},{96,128},{128,160},{160,192},{192,224},{224... | collective-permute-start | bytes 786440 | tf_op jit(solution)/shard_map/while/body/eval_jaxpr/ppermute | solution.py:17
  194.7 8.4 %collective-permute-start.1 = (bf16[1024,128]{1,0:T(8,128)(2,1)}, bf16[1024,128]{1,0:T(8,128)(2,1)S(1)}, u32[]{:S(2)}, u32[]{:S(2)}) collective-permute-start(bf16[1024,128]{1,0:T(8,128)(2,1)} %copy.35), channel_id=1, source_target_pairs={{0,32},{32,64},{64,96},{96,128},{128,160},{160,192},{192,224},{224... | collective-permute-start | bytes 786440 | tf_op jit(solution)/shard_map/while/body/eval_jaxpr/ppermute | solution.py:17
  203.9 12.8 %collective-permute-start = (bf16[1024,128]{1,0:T(8,128)(2,1)}, bf16[1024,128]{1,0:T(8,128)(2,1)S(1)}, u32[]{:S(2)}, u32[]{:S(2)}) collective-permute-start(bf16[1024,128]{1,0:T(8,128)(2,1)} %copy.34), channel_id=1, source_target_pairs={{0,32},{32,64},{64,96},{96,128},{128,160},{160,192},{192,224},{224... | collective-permute-start | bytes 786440 | tf_op jit(solution)/shard_map/while/body/eval_jaxpr/ppermute | solution.py:17
  207.7 8.9 %collective-permute-start.1 = (bf16[1024,128]{1,0:T(8,128)(2,1)}, bf16[1024,128]{1,0:T(8,128)(2,1)S(1)}, u32[]{:S(2)}, u32[]{:S(2)}) collective-permute-start(bf16[1024,128]{1,0:T(8,128)(2,1)} %copy.35), channel_id=1, source_target_pairs={{0,32},{32,64},{64,96},{96,128},{128,160},{160,192},{192,224},{224... | collective-permute-start | bytes 786440 | tf_op jit(solution)/shard_map/while/body/eval_jaxpr/ppermute | solution.py:17
  217.4 14.0 %collective-permute-start = (bf16[1024,128]{1,0:T(8,128)(2,1)}, bf16[1024,128]{1,0:T(8,128)(2,1)S(1)}, u32[]{:S(2)}, u32[]{:S(2)}) collective-permute-start(bf16[1024,128]{1,0:T(8,128)(2,1)} %copy.34), channel_id=1, source_target_pairs={{0,32},{32,64},{64,96},{96,128},{128,160},{160,192},{192,224},{224... | collective-permute-start | bytes 786440 | tf_op jit(solution)/shard_map/while/body/eval_jaxpr/ppermute | solution.py:17
  222.5 8.9 %collective-permute-start.1 = (bf16[1024,128]{1,0:T(8,128)(2,1)}, bf16[1024,128]{1,0:T(8,128)(2,1)S(1)}, u32[]{:S(2)}, u32[]{:S(2)}) collective-permute-start(bf16[1024,128]{1,0:T(8,128)(2,1)} %copy.35), channel_id=1, source_target_pairs={{0,32},{32,64},{64,96},{96,128},{128,160},{160,192},{192,224},{224... | collective-permute-start | bytes 786440 | tf_op jit(solution)/shard_map/while/body/eval_jaxpr/ppermute | solution.py:17
  232.1 12.8 %collective-permute-start = (bf16[1024,128]{1,0:T(8,128)(2,1)}, bf16[1024,128]{1,0:T(8,128)(2,1)S(1)}, u32[]{:S(2)}, u32[]{:S(2)}) collective-permute-start(bf16[1024,128]{1,0:T(8,128)(2,1)} %copy.34), channel_id=1, source_target_pairs={{0,32},{32,64},{64,96},{96,128},{128,160},{160,192},{192,224},{224... | collective-permute-start | bytes 786440 | tf_op jit(solution)/shard_map/while/body/eval_jaxpr/ppermute | solution.py:17
  236.0 8.9 %collective-permute-start.1 = (bf16[1024,128]{1,0:T(8,128)(2,1)}, bf16[1024,128]{1,0:T(8,128)(2,1)S(1)}, u32[]{:S(2)}, u32[]{:S(2)}) collective-permute-start(bf16[1024,128]{1,0:T(8,128)(2,1)} %copy.35), channel_id=1, source_target_pairs={{0,32},{32,64},{64,96},{96,128},{128,160},{160,192},{192,224},{224... | collective-permute-start | bytes 786440 | tf_op jit(solution)/shard_map/while/body/eval_jaxpr/ppermute | solution.py:17
  245.6 16.3 %collective-permute-start = (bf16[1024,128]{1,0:T(8,128)(2,1)}, bf16[1024,128]{1,0:T(8,128)(2,1)S(1)}, u32[]{:S(2)}, u32[]{:S(2)}) collective-permute-start(bf16[1024,128]{1,0:T(8,128)(2,1)} %copy.34), channel_id=1, source_target_pairs={{0,32},{32,64},{64,96},{96,128},{128,160},{160,192},{192,224},{224... | collective-permute-start | bytes 786440 | tf_op jit(solution)/shard_map/while/body/eval_jaxpr/ppermute | solution.py:17
  249.5 12.5 %collective-permute-start.1 = (bf16[1024,128]{1,0:T(8,128)(2,1)}, bf16[1024,128]{1,0:T(8,128)(2,1)S(1)}, u32[]{:S(2)}, u32[]{:S(2)}) collective-permute-start(bf16[1024,128]{1,0:T(8,128)(2,1)} %copy.35), channel_id=1, source_target_pairs={{0,32},{32,64},{64,96},{96,128},{128,160},{160,192},{192,224},{224... | collective-permute-start | bytes 786440 | tf_op jit(solution)/shard_map/while/body/eval_jaxpr/ppermute | solution.py:17
  262.7 12.8 %collective-permute-start = (bf16[1024,128]{1,0:T(8,128)(2,1)}, bf16[1024,128]{1,0:T(8,128)(2,1)S(1)}, u32[]{:S(2)}, u32[]{:S(2)}) collective-permute-start(bf16[1024,128]{1,0:T(8,128)(2,1)} %copy.34), channel_id=1, source_target_pairs={{0,32},{32,64},{64,96},{96,128},{128,160},{160,192},{192,224},{224... | collective-permute-start | bytes 786440 | tf_op jit(solution)/shard_map/while/body/eval_jaxpr/ppermute | solution.py:17
  265.3 10.2 %collective-permute-start.1 = (bf16[1024,128]{1,0:T(8,128)(2,1)}, bf16[1024,128]{1,0:T(8,128)(2,1)S(1)}, u32[]{:S(2)}, u32[]{:S(2)}) collective-permute-start(bf16[1024,128]{1,0:T(8,128)(2,1)} %copy.35), channel_id=1, source_target_pairs={{0,32},{32,64},{64,96},{96,128},{128,160},{160,192},{192,224},{224... | collective-permute-start | bytes 786440 | tf_op jit(solution)/shard_map/while/body/eval_jaxpr/ppermute | solution.py:17
  277.3 3.2 %collective-permute-start.6 = (bf16[512,128]{1,0:T(8,128)(2,1)S(1)}, bf16[512,128]{1,0:T(8,128)(2,1)S(1)}, u32[]{:S(2)}, u32[]{:S(2)}) collective-permute-start(bf16[512,128]{1,0:T(8,128)(2,1)S(1)} %divide_convert_fusion), channel_id=1, source_target_pairs={{0,32},{32,0},{64,96},{96,64},{128,160},{160,128},{192,224},{224,1... | collective-permute-start | bytes 393224 | tf_op jit(solution)/shard_map/ppermute | solution.py:12
  280.6 7.4 %collective-permute-start.7 = (bf16[512,128]{1,0:T(8,128)(2,1)S(1)}, bf16[512,128]{1,0:T(8,128)(2,1)S(1)}, u32[]{:S(2)}, u32[]{:S(2)}) collective-permute-start(bf16[512,128]{1,0:T(8,128)(2,1)S(1)} %collective-permute-done.6), channel_id=1, source_target_pairs={{0,64},{32,96},{64,0},{96,32},{128,192},{160,224},{192,128},{224,1... | collective-permute-start | bytes 393224 | tf_op jit(solution)/shard_map/ppermute | solution.py:12
  288.0 8.4 %collective-permute-start.8 = (bf16[512,128]{1,0:T(8,128)(2,1)S(1)}, bf16[512,128]{1,0:T(8,128)(2,1)S(1)}, u32[]{:S(2)}, u32[]{:S(2)}) collective-permute-start(bf16[512,128]{1,0:T(8,128)(2,1)S(1)} %collective-permute-done.7), channel_id=1, source_target_pairs={{0,128},{32,160},{64,192},{96,224},{128,0},{160,32},{192,64},{224,... | collective-permute-start | bytes 393224 | tf_op jit(solution)/shard_map/ppermute | solution.py:12
  296.4 6.8 %collective-permute-start.9 = (bf16[512,128]{1,0:T(8,128)(2,1)S(1)}, bf16[512,128]{1,0:T(8,128)(2,1)S(1)}, u32[]{:S(2)}, u32[]{:S(2)}) collective-permute-start(bf16[512,128]{1,0:T(8,128)(2,1)S(1)} %collective-permute-done.8), channel_id=1, source_target_pairs={{0,256},{32,288},{64,320},{96,352},{128,384},{160,416},{192,448},{... | collective-permute-start | bytes 393224 | tf_op jit(solution)/shard_map/ppermute | solution.py:12
where the time goes:
time: 307 us; the launch traced here: 304 us
  starting transfers between devices  131 us (43%)
  matrix products  49.5 us (16%)
  waiting for transfers between devices  46.3 us (15%)
  local copies, waits for them, and re-layouts  44.8 us (15%)
  loops' own time  20.4 us (7%)
  other arithmetic  10.1 us (3%)
    ppermute x30, starting transfers between devices, from_behind(): lax.ppermute(shard, axis, [(i, (i + by) % length) for i in range(length)])  92.5 us
    ppermute x8, waiting for transfers between devices, swapped(): return lax.ppermute(value, axis, pairs)  28.2 us
    dot_general x17, matrix products, compute(): jnp.dot(weights.astype(jnp.bfloat16), block_values, preferred_element_typ...  24.8 us
    dot_general x17, matrix products, compute(): lax.dot_general(query_block, block_keys, (((1,), (1,)), ((), ())), prefer...  24.6 us
    while x30, local copies, waits for them, and re-layouts  21 us
    another operation x1, loops' own time, per_device(): lax.fori_loop(0, cycle_size - 1, turn, (states, own_keys, own_values))  19.6 us
    slice x32, local copies, waits for them, and re-layouts, update(): needed = source * row_count <= query_pos[half_rows - 1]  19.6 us
    ppermute x8, starting transfers between devices, swapped(): return lax.ppermute(value, axis, pairs)  18.9 us
  transfers between devices with their start and end apart: 40, of which 11 were waited for; matrix products, arithmetic and copies ran while one was open for 30% of the time, Pallas kernels for 0%

commit v1 on v0

v1 whole, which is shorter than its diff:
```python
import functools
import math

import jax
import jax.numpy as jnp
from jax import lax
from jax.experimental import pallas as pl
from jax.experimental.pallas import tpu as pltpu
from jax.sharding import PartitionSpec as P

MESH = pl.DeviceIdType.MESH
NEG = -1e30
BLOCKS = 16
QT = 256
XP, XM, X2, SIB, UP, SIB_XP, SIB_XM, SIB_X2, Y_X2, SIB_UP, Y = range(11)


def kernel(q_ref, k_ref, v_ref, o_ref, kv, stage, wide, qc, qh, oh, lh, lh_out, m, l, acc,
           ss, rs, p1s, p1r, qsem, osem, lsem):
    c = lax.axis_index("ctx")
    h = lax.axis_index("head")
    z, x, core = c // 8, (c // 2) % 4, c % 2
    group, lane = h // 4, h % 4
    rows = q_ref.shape[0]
    tiles = rows // QT

    def quarter(r):
        return (lane + r) % 2 + 2 * ((lane // 2 + r // 2) % 2)

    def device(x_, z_, core_, lane_):
        return {"ctx": z_ * 8 + x_ * 2 + core_, "head": group * 4 + lane_}

    xp, xm, x2 = (x + 1) % 4, (x + 3) % 4, (x + 2) % 4
    to_xp, to_xm, to_x2 = (device(t, z, core, lane) for t in (xp, xm, x2))
    to_sib = device(x, z, 1 - core, lane)
    to_z = device(x, 1 - z, core, lane)
    to_mirror = device(3 - x, 1 - z, 1 - core, lane)
    to_y = [None] + [device(x, z, core, quarter(r)) for r in (1, 2, 3)]
    to_group = [None] + [{"ctx": c, "head": ((group + d) % 8) * 4 + lane} for d in range(1, 8)]

    barrier = pltpu.get_barrier_semaphore()
    partners = to_group[1:] + to_y[1:] + [to_xp, to_xm, to_x2, to_sib, to_z, to_mirror]
    for partner in partners:
        pl.semaphore_signal(barrier, inc=1, device_id=partner, device_id_type=MESH)

    for ref, first in ((k_ref, 0), (v_ref, 32)):
        wide[...] = ref[...].astype(jnp.float32).reshape(wide.shape)
        for g in range(8):
            stage[g, first:first + 32] = wide[pl.ds(g, 32, stride=8), :].astype(jnp.bfloat16)
    kv[c, lane, group] = stage[group]

    scale = math.log2(math.e) / math.sqrt(q_ref.shape[1])

    def split_scaled(job, src):
        def one(i, _):
            r = pl.ds(pl.multiple_of(i * QT, QT), QT)
            scaled = src[r].astype(jnp.float32) * scale
            high = scaled.astype(jnp.bfloat16)
            qc[job, r, :128] = high
            qc[job, r, 128:] = (scaled - high.astype(jnp.float32)).astype(jnp.bfloat16)
            return 0
        lax.fori_loop(0, tiles, one, 0)

    split_scaled(0, q_ref)
    m[...] = jnp.full(m.shape, NEG, jnp.float32)
    l[...] = jnp.zeros(l.shape, jnp.float32)
    acc[...] = jnp.zeros(acc.shape, jnp.float32)

    pl.semaphore_wait(barrier, len(partners))

    def remote(src, dst, send, recv, to):
        return pltpu.make_async_remote_copy(
            src_ref=src, dst_ref=dst, send_sem=send, recv_sem=recv, device_id=to, device_id_type=MESH)

    def scatter(d):
        return remote(stage.at[(group + d) % 8], kv.at[c, lane, group], p1s.at[d], p1r.at[d], to_group[d])

    for d in (4, 3, 5, 2, 6, 1, 7):
        scatter(d).start()
    query_copy = remote(q_ref, qh, qsem.at[0], qsem.at[1], to_mirror)

    @pl.when(z == 1)
    def _():
        query_copy.start()

    def piece(kind, r, block, to):
        q = quarter(r)
        return remote(kv.at[block, q], kv.at[block, q], ss.at[kind, r], rs.at[block, q], to)

    def landed(r, block):
        piece(0, r, block, to_sib).wait_recv()

    def from_chip(x_):
        return 2 * x_ + 8 * z * (x_ < x).astype(jnp.int32)

    is_late = z == 1
    own_up = 2 * x + core
    own_goes = {XP: (z == 0) | (x < 3), XM: (z == 0) | (x < 1), X2: (z == 0) | (x < 2)}
    targets = {XP: to_xp, XM: to_xm, X2: to_x2}

    def kinds_x(r_even):
        return (XP, XM, X2) if r_even else (XP, XM)

    def own_quarter(r, r_even, first=False):
        if not first:
            landed(r, c)
        for kind in kinds_x(r_even):
            @pl.when(own_goes[kind])
            def _(kind=kind):
                piece(kind, r, c, targets[kind]).start()

        @pl.when(z == 0)
        def _():
            piece(UP, r, c, to_z).start()

        piece(SIB, r, c, to_sib).start()

    def up_quarter(r, r_even):
        @pl.when(is_late)
        def _():
            landed(r, own_up)
            for kind in kinds_x(r_even):
                @pl.when(jnp.logical_not(own_goes[kind]))
                def _(kind=kind):
                    piece(kind, r, own_up, targets[kind]).start()
            piece(SIB_UP, r, own_up, to_sib).start()

    def x_quarters(r):
        for kind, source in ((SIB_XP, xp), (SIB_XM, xm)):
            landed(r, from_chip(source) + core)
            piece(kind, r, from_chip(source) + core, to_sib).start()

    def x2_quarter(r, r_even):
        block = from_chip(x2) + core
        landed(r, block)
        if r_even:
            piece(Y_X2, r, block, to_y[1]).start()
        piece(SIB_X2, r, block, to_sib).start()

    def sib_near(r):
        landed(r, c + 1 - 2 * core)

        @pl.when(is_late)
        def _():
            landed(r, own_up + 1 - 2 * core)
        landed(r, from_chip(xp) + 1 - core)
        landed(r, from_chip(xm) + 1 - core)

    def sib_far(r):
        landed(r, from_chip(x2) + 1 - core)

    def attend(job, tile, keys, values, mask=None):
        at = slice(tile * QT, (tile + 1) * QT)
        scores = lax.dot_general(qc[job, at], jnp.concatenate([keys, keys], axis=1),
                                 (((1,), (1,)), ((), ())), preferred_element_type=jnp.float32)
        if mask is not None:
            scores = jnp.where(mask, scores, NEG)
        before = m[job, at]
        now = jnp.maximum(before, jnp.max(scores, axis=1, keepdims=True))
        shrink = jnp.exp2(before - now)
        weights = jnp.exp2(scores - now[:, :1]).astype(jnp.bfloat16)
        mixed = jnp.dot(weights, jnp.concatenate([values, jnp.ones_like(values)], axis=1),
                        preferred_element_type=jnp.float32)
        m[job, at] = now
        acc[job, at] = acc[job, at] * shrink + mixed[:, :128]
        l[job, at] = l[job, at] * shrink + mixed[:, 128:]

    def load(blocks, half, first, count):
        parts = [(b, quarter(2 * half + i)) for b in blocks for i in range(2)]
        def side(at):
            return jnp.concatenate(
                [kv[b, q, pl.ds(first, count), at:at + 32, :].reshape(count * 32, 128) for b, q in parts], axis=0)
        return side(0), side(32)

    def diagonal(half):
        for tile in range(tiles):
            count = 2 * (tile + 1)
            keys, values = load([c], half, 0, count)
            spot = lax.broadcasted_iota(jnp.int32, (1, count * 64), 1)
            which = jnp.where(spot < count * 32, quarter(2 * half), quarter(2 * half + 1))
            inner = spot % (count * 32)
            key_pos = (inner // 32) * 128 + which * 32 + inner % 32
            query_pos = tile * QT + lax.broadcasted_iota(jnp.int32, (QT, 1), 0)
            attend(0, tile, keys, values, key_pos <= query_pos)

    def single_and_half(half):
        early = 1 - z
        block = jnp.where(is_late, 2 * x + jnp.where(core == 0, 1, 8), jnp.where(core == 0, 6 - 2 * x, 2 * x))
        job = jnp.where(core == 0, early, 0)
        keys, values = load([block], half, 0, 8)
        for tile in range(tiles):
            attend(job, tile, keys, values)
        block = jnp.where(is_late, 2 * x + core, 7 - 2 * x - core)
        keys, values = load([block], half, 4 * z, 4)
        for tile in range(tiles):
            attend(early, tile, keys, values)

    def by_x(a0, a1, a2, a3):
        return jnp.where(x == 0, a0, jnp.where(x == 1, a1, jnp.where(x == 2, a2, a3)))

    def by_step(i, a0, a1, a2):
        return jnp.where(i == 0, a0, jnp.where(i == 1, a1, a2))

    def pair(i, half):
        late_chip = by_step(i, xp, xm, x2)
        early_chip = by_step(i, by_x(0, 1, 1, 0), by_x(1, 0, 0, 2), by_x(2, 0, 0, 1))
        early_job = by_step(i, by_x(1, 1, 0, 0), by_x(1, 0, 0, 0), by_x(1, 1, 1, 0))
        base = from_chip(jnp.where(is_late, late_chip, early_chip))
        job = jnp.where(is_late, 0, early_job)
        keys, values = load([base, base + 1], half, 0, 8)
        for tile in range(tiles):
            attend(job, tile, keys, values)

    for d in range(1, 8):
        scatter(d).wait_recv()
    for step in (1, 2, 3):
        piece_y = remote(kv.at[c, lane], kv.at[c, lane], ss.at[Y, step], rs.at[c, lane], to_y[step])
        piece_y.start()
    own_quarter(0, True, True)
    up_quarter(0, True)
    x_quarters(0)
    own_quarter(1, False)

    @pl.when(z == 0)
    def _():
        query_copy.wait_recv()
        split_scaled(1, qh)

    def both(half, _):
        first = half == 0
        r0, r1 = 2 * half, 2 * half + 1
        diagonal(half)

        @pl.when(first)
        def _():
            x2_quarter(0, True)
        up_quarter(r1, False)
        x_quarters(r1)

        @pl.when(first)
        def _():
            own_quarter(2, True)
        sib_near(r0)
        sib_near(r1)
        single_and_half(half)

        @pl.when(first)
        def _():
            own_quarter(3, False)
            up_quarter(2, True)
            x_quarters(2)

        def one(i, _):
            @pl.when(i == 1)
            def _():
                x2_quarter(r1, False)
                sib_far(r0)
                sib_far(r1)

            pair(i, half)

            @pl.when((i == 1) & first)
            def _():
                x2_quarter(2, True)
            return 0
        lax.fori_loop(0, 3, one, 0)
        return 0

    lax.fori_loop(0, 2, both, 0)

    eye = (lax.broadcasted_iota(jnp.int32, (128, 128), 0) == lax.broadcasted_iota(jnp.int32, (128, 128), 1))
    out_copy = remote(oh, qh, osem.at[0], osem.at[1], to_mirror)
    log_copy = remote(lh_out, lh, lsem.at[0], lsem.at[1], to_mirror)

    @pl.when(z == 0)
    def _():
        for i in range(rows // 128):
            at = slice(i * 128, (i + 1) * 128)
            oh[at] = (acc[1, at] / l[1, at]).astype(jnp.bfloat16)
            log = m[1, at] + jnp.log2(l[1, at])
            lh_out[i:i + 1] = jnp.sum(jnp.where(eye, log, 0.0), axis=0, keepdims=True)
        log_copy.start()
        out_copy.start()
        o_ref[...] = (acc[0] / l[0]).astype(jnp.bfloat16)

    @pl.when(z == 1)
    def _():
        query_copy.wait_send()
        log_copy.wait_recv()
        out_copy.wait_recv()
        for i in range(rows // 128):
            at = slice(i * 128, (i + 1) * 128)
            log = jnp.sum(jnp.where(eye, lh[i:i + 1], 0.0), axis=1, keepdims=True)
            mine = m[0, at]
            top = jnp.maximum(mine, log)
            w_mine, w_help = jnp.exp2(mine - top), jnp.exp2(log - top)
            total = l[0, at] * w_mine + w_help
            mixed = acc[0, at] * w_mine + qh[at].astype(jnp.float32) * w_help
            o_ref[at] = (mixed / total).astype(jnp.bfloat16)

    @pl.when(z == 0)
    def _():
        log_copy.wait_send()
        out_copy.wait_send()
    for d in range(1, 8):
        scatter(d).wait_send()
    for r in range(4):
        kinds = [XP, XM, SIB, SIB_XP, SIB_XM, SIB_X2] + ([X2, Y_X2] if r % 2 == 0 else []) + ([Y] if r else [])
        for kind in kinds:
            piece(kind, r, c, to_sib).wait_send()
        for kind, when in ((UP, z == 0), (SIB_UP, z == 1)):
            @pl.when(when)
            def _(kind=kind):
                piece(kind, r, c, to_sib).wait_send()


def per_device(queries, key_states, value_states):
    rows, _, width = queries.shape
    f32, bf16 = jnp.float32, jnp.bfloat16
    dma = pltpu.SemaphoreType.DMA
    out = pl.pallas_call(
        kernel,
        out_shape=jax.ShapeDtypeStruct((rows, width), bf16),
        in_specs=[pl.BlockSpec(memory_space=pltpu.VMEM)] * 3,
        out_specs=pl.BlockSpec(memory_space=pltpu.VMEM),
        scratch_shapes=[
            pltpu.VMEM((BLOCKS, 4, 8, 64, width), bf16),
            pltpu.VMEM((8, 64, width), bf16),
            pltpu.VMEM((256, width), f32),
            pltpu.VMEM((2, rows, 2 * width), bf16),
            pltpu.VMEM((rows, width), bf16),
            pltpu.VMEM((rows, width), bf16),
            pltpu.VMEM((8, 128), f32),
            pltpu.VMEM((8, 128), f32),
            pltpu.VMEM((2, rows, width), f32),
            pltpu.VMEM((2, rows, width), f32),
            pltpu.VMEM((2, rows, width), f32),
            dma((11, 4)),
            dma((BLOCKS, 4)),
            dma((8,)),
            dma((8,)),
            dma((2,)),
            dma((2,)),
            dma((2,)),
        ],
        name="folded_attention",
        cost_estimate=pl.CostEstimate(flops=4 * 128 * 8 * 1024 * 1024, bytes_accessed=2**20, transcendentals=2**23),
        compiler_params=pltpu.CompilerParams(
            collective_id=0, has_side_effects=True, vmem_limit_bytes=48 * 2**20),
    )(queries.reshape(rows, width), key_states, value_states)
    return out[:, None, :]


def solution(mesh):
    return jax.shard_map(
        per_device,
        mesh=mesh,
        in_specs=(
            P("ctx", "head", None),
            P(("ctx", "head"), None, None),
            P(("ctx", "head"), None, None),
        ),
        out_specs=P("ctx", "head", None),
        check_vma=False,
    )
```

time: 307 us -> 77.9 us (0.25)
  the two profiles are of different devices: /device:TPU:6 before, /device:TPU:64 now
where the time goes in v1:
time: 77.9 us; the launch traced here: 77.6 us
  Pallas kernels  74.3 us (95%)
  local copies, waits for them, and re-layouts  3.33 us (4%)
    pallas_call x1, Pallas kernels, per_device(): pl.pallas_call(kernel, out_shape=jax.ShapeDtypeStruct((rows, width), bf16...  74.3 us
    unnamed x7, local copies, waits for them, and re-layouts  3.33 us

profile of v1, /device:TPU:64, one launch (start us, length us, event | category | flops | bytes accessed | tf_op | source)
XLA Modules:
  0.0 77.6 jit_solution(7593965549992013784)
XLA Ops:
  0.0 0.0 copy-start
  0.0 0.9 %copy-done = bf16[1024,1,128]{2,0,1:T(8,128)(2,1)S(1)} copy-done((bf16[1024,1,128]{2,0,1:T(8,128)(2,1)S(1)}, bf16[1024,1,128]{2,0,1:T(8,128)(2,1)}, u32[]{:S(2)}) %copy-start) | copy-done | bytes 262168
  1.0 0.0 copy-start.1
  1.0 0.8 %copy-done.1 = bf16[32,8,128]{2,1,0:T(8,128)(2,1)S(1)} copy-done((bf16[32,8,128]{2,1,0:T(8,128)(2,1)S(1)}, bf16[32,8,128]{2,1,0:T(8,128)(2,1)}, u32[]{:S(2)}) %copy-start.1) | copy-done | bytes 65560
  1.8 0.0 copy-start.2
  1.8 0.8 %copy-done.2 = bf16[32,8,128]{2,1,0:T(8,128)(2,1)S(1)} copy-done((bf16[32,8,128]{2,1,0:T(8,128)(2,1)S(1)}, bf16[32,8,128]{2,1,0:T(8,128)(2,1)}, u32[]{:S(2)}) %copy-start.2) | copy-done | bytes 65560
  2.6 74.3 %folded_attention.1 = bf16[1024,128]{1,0:T(8,128)(2,1)S(1)} custom-call(bf16[1024,128]{1,0:T(8,128)(2,1)S(1)} %bitcast.3, bf16[32,8,128]{2,1,0:T(8,128)(2,1)S(1)} %copy-done.1, bf16[32,8,128]{2,1,0:T(8,128)(2,1)S(1)} %copy-done.2), custom_call_target="tpu_custom_call" | custom-call | flops 4294967296 | bytes 1048576 | tf_op jit(solution)/shard_map/folded_attention/pallas_call | solution.py:321
  76.9 0.7 copy.5
Async XLA Ops:
  0.0 0.9 %copy-start = (bf16[1024,1,128]{2,0,1:T(8,128)(2,1)S(1)}, bf16[1024,1,128]{2,0,1:T(8,128)(2,1)}, u32[]{:S(2)}) copy-start(bf16[1024,1,128]{2,0,1:T(8,128)(2,1)} %param.3) | copy-start | bytes 786436
  1.0 0.8 %copy-start.1 = (bf16[32,8,128]{2,1,0:T(8,128)(2,1)S(1)}, bf16[32,8,128]{2,1,0:T(8,128)(2,1)}, u32[]{:S(2)}) copy-start(bf16[32,8,128]{2,1,0:T(8,128)(2,1)} %k_ref.1) | copy-start | bytes 196612
  1.8 0.8 %copy-start.2 = (bf16[32,8,128]{2,1,0:T(8,128)(2,1)S(1)}, bf16[32,8,128]{2,1,0:T(8,128)(2,1)}, u32[]{:S(2)}) copy-start(bf16[32,8,128]{2,1,0:T(8,128)(2,1)} %v_ref.1) | copy-start | bytes 196612

commit v2 on v1

--- a/solution.py
+++ b/solution.py
@@ -15,8 +15,8 @@
 XP, XM, X2, SIB, UP, SIB_XP, SIB_XM, SIB_X2, Y_X2, SIB_UP, Y = range(11)
 
 
-def kernel(q_ref, k_ref, v_ref, o_ref, kv, stage, wide, qc, qh, oh, lh, lh_out, m, l, acc,
-           ss, rs, p1s, p1r, qsem, osem, lsem):
+def kernel(q_hbm, k_hbm, v_hbm, o_ref, q_ref, k_ref, v_ref, kv, stage, wide, qc, qh, oh, lh, lh_out, m, l, acc,
+           ss, rs, p1s, p1r, qsem, osem, lsem, isem):
     c = lax.axis_index("ctx")
     h = lax.axis_index("head")
     z, x, core = c // 8, (c // 2) % 4, c % 2
@@ -42,6 +42,13 @@
     partners = to_group[1:] + to_y[1:] + [to_xp, to_xm, to_x2, to_sib, to_z, to_mirror]
     for partner in partners:
         pl.semaphore_signal(barrier, inc=1, device_id=partner, device_id_type=MESH)
+
+    loads = [pltpu.make_async_copy(src, dst, isem.at[i])
+             for i, (src, dst) in enumerate(((k_hbm, k_ref), (v_hbm, v_ref), (q_hbm, q_ref)))]
+    for copy in loads:
+        copy.start()
+    loads[0].wait()
+    loads[1].wait()
 
     for ref, first in ((k_ref, 0), (v_ref, 32)):
         wide[...] = ref[...].astype(jnp.float32).reshape(wide.shape)
@@ -61,6 +68,7 @@
             return 0
         lax.fori_loop(0, tiles, one, 0)
 
+    loads[2].wait()
     split_scaled(0, q_ref)
     m[...] = jnp.full(m.shape, NEG, jnp.float32)
     l[...] = jnp.zeros(l.shape, jnp.float32)
@@ -104,14 +112,14 @@
     def own_quarter(r, r_even, first=False):
         if not first:
             landed(r, c)
+        @pl.when(z == 0)
+        def _():
+            piece(UP, r, c, to_z).start()
+
         for kind in kinds_x(r_even):
             @pl.when(own_goes[kind])
             def _(kind=kind):
                 piece(kind, r, c, targets[kind]).start()
-
-        @pl.when(z == 0)
-        def _():
-            piece(UP, r, c, to_z).start()
 
         piece(SIB, r, c, to_sib).start()
 
@@ -137,33 +145,41 @@
             piece(Y_X2, r, block, to_y[1]).start()
         piece(SIB_X2, r, block, to_sib).start()
 
-    def sib_near(r):
+    def sib_own(r):
         landed(r, c + 1 - 2 * core)
 
-        @pl.when(is_late)
-        def _():
-            landed(r, own_up + 1 - 2 * core)
+    def sib_up(r):
+        landed(r, own_up + 1 - 2 * core)
+
+    def sib_x(r):
         landed(r, from_chip(xp) + 1 - core)
         landed(r, from_chip(xm) + 1 - core)
 
-    def sib_far(r):
+    def sib_x2(r):
         landed(r, from_chip(x2) + 1 - core)
 
-    def attend(job, tile, keys, values, mask=None):
-        at = slice(tile * QT, (tile + 1) * QT)
-        scores = lax.dot_general(qc[job, at], jnp.concatenate([keys, keys], axis=1),
-                                 (((1,), (1,)), ((), ())), preferred_element_type=jnp.float32)
-        if mask is not None:
-            scores = jnp.where(mask, scores, NEG)
-        before = m[job, at]
-        now = jnp.maximum(before, jnp.max(scores, axis=1, keepdims=True))
-        shrink = jnp.exp2(before - now)
-        weights = jnp.exp2(scores - now[:, :1]).astype(jnp.bfloat16)
-        mixed = jnp.dot(weights, jnp.concatenate([values, jnp.ones_like(values)], axis=1),
-                        preferred_element_type=jnp.float32)
-        m[job, at] = now
-        acc[job, at] = acc[job, at] * shrink + mixed[:, :128]
-        l[job, at] = l[job, at] * shrink + mixed[:, 128:]
+    def attend(job, parts):
+        scores = []
+        for tile, (keys, values, mask) in enumerate(parts):
+            at = slice(tile * QT, (tile + 1) * QT)
+            score = lax.dot_general(qc[job, at], jnp.concatenate([keys, keys], axis=1),
+                                    (((1,), (1,)), ((), ())), preferred_element_type=jnp.float32)
+            scores.append(score if mask is None else jnp.where(mask, score, NEG))
+        rounded, shrinks = [], []
+        for tile, score in enumerate(scores):
+            at = slice(tile * QT, (tile + 1) * QT)
+            before = m[job, at]
+            now = jnp.maximum(before, jnp.max(score, axis=1, keepdims=True))
+            m[job, at] = now
+            shrinks.append(jnp.exp2(before - now))
+            across = jnp.concatenate([now] * (score.shape[1] // 128), axis=1)
+            rounded.append(jnp.exp2(score - across).astype(jnp.bfloat16))
+        for tile, (_, values, _) in enumerate(parts):
+            at = slice(tile * QT, (tile + 1) * QT)
+            mixed = jnp.dot(rounded[tile], jnp.concatenate([values, jnp.ones_like(values)], axis=1),
+                            preferred_element_type=jnp.float32)
+            acc[job, at] = acc[job, at] * shrinks[tile] + mixed[:, :128]
+            l[job, at] = l[job, at] * shrinks[tile] + mixed[:, 128:]
 
     def load(blocks, half, first, count):
         parts = [(b, quarter(2 * half + i)) for b in blocks for i in range(2)]
@@ -173,6 +189,7 @@
         return side(0), side(32)
 
     def diagonal(half):
+        parts = []
         for tile in range(tiles):
             count = 2 * (tile + 1)
             keys, values = load([c], half, 0, count)
@@ -181,19 +198,12 @@
             inner = spot % (count * 32)
             key_pos = (inner // 32) * 128 + which * 32 + inner % 32
             query_pos = tile * QT + lax.broadcasted_iota(jnp.int32, (QT, 1), 0)
-            attend(0, tile, keys, values, key_pos <= query_pos)
-
-    def single_and_half(half):
-        early = 1 - z
-        block = jnp.where(is_late, 2 * x + jnp.where(core == 0, 1, 8), jnp.where(core == 0, 6 - 2 * x, 2 * x))
-        job = jnp.where(core == 0, early, 0)
-        keys, values = load([block], half, 0, 8)
-        for tile in range(tiles):
-            attend(job, tile, keys, values)
-        block = jnp.where(is_late, 2 * x + core, 7 - 2 * x - core)
-        keys, values = load([block], half, 4 * z, 4)
-        for tile in range(tiles):
-            attend(early, tile, keys, values)
+            parts.append((keys, values, key_pos <= query_pos))
+        attend(0, parts)
+
+    def single(half):
+        keys, values = load([jnp.where(core == 0, 6 - 2 * x, 2 * x)], half, 0, 8)
+        attend(1 - core, [(keys, values, None)] * tiles)
 
     def by_x(a0, a1, a2, a3):
         return jnp.where(x == 0, a0, jnp.where(x == 1, a1, jnp.where(x == 2, a2, a3)))
@@ -202,14 +212,18 @@
         return jnp.where(i == 0, a0, jnp.where(i == 1, a1, a2))
 
     def pair(i, half):
-        late_chip = by_step(i, xp, xm, x2)
-        early_chip = by_step(i, by_x(0, 1, 1, 0), by_x(1, 0, 0, 2), by_x(2, 0, 0, 1))
-        early_job = by_step(i, by_x(1, 1, 0, 0), by_x(1, 0, 0, 0), by_x(1, 1, 1, 0))
-        base = from_chip(jnp.where(is_late, late_chip, early_chip))
-        job = jnp.where(is_late, 0, early_job)
-        keys, values = load([base, base + 1], half, 0, 8)
-        for tile in range(tiles):
-            attend(job, tile, keys, values)
+        late_base = from_chip(by_step(i - 1, xp, xm, x2))
+        late_a = jnp.where(i == 0, own_up, late_base)
+        late_b = jnp.where(i == 0, 2 * x + jnp.where(core == 0, 1, 8), late_base + 1)
+        chip_a = by_step(i - 1, by_x(0, 1, 1, 0), by_x(1, 0, 0, 2), by_x(2, 0, 0, 1))
+        job_a = by_step(i - 1, by_x(1, 1, 0, 0), by_x(1, 0, 0, 0), by_x(1, 1, 1, 0))
+        chip_b = by_step(i - 1, by_x(0, 1, 0, 0), by_x(1, 0, 1, 2), by_x(2, 0, 0, 1))
+        job_b = by_step(i - 1, by_x(1, 1, 1, 0), by_x(1, 1, 0, 0), by_x(1, 0, 0, 0))
+        early_a = 2 * jnp.where(half == 0, chip_a, chip_b)
+        job = jnp.where(is_late, 0, jnp.where(half == 0, job_a, job_b))
+        blocks = [jnp.where(is_late, late_a, early_a), jnp.where(is_late, late_b, early_a + 1)]
+        keys, values = load(blocks, half, 0, 8)
+        attend(job, [(keys, values, None)] * tiles)
 
     for d in range(1, 8):
         scatter(d).wait_recv()
@@ -217,15 +231,31 @@
         piece_y = remote(kv.at[c, lane], kv.at[c, lane], ss.at[Y, step], rs.at[c, lane], to_y[step])
         piece_y.start()
     own_quarter(0, True, True)
-    up_quarter(0, True)
-    x_quarters(0)
-    own_quarter(1, False)
 
     @pl.when(z == 0)
     def _():
         query_copy.wait_recv()
         split_scaled(1, qh)
 
+    up_quarter(0, True)
+    x_quarters(0)
+    own_quarter(1, False)
+
+    eye = (lax.broadcasted_iota(jnp.int32, (128, 128), 0) == lax.broadcasted_iota(jnp.int32, (128, 128), 1))
+    out_copy = remote(oh, qh, osem.at[0], osem.at[1], to_mirror)
+    log_copy = remote(lh_out, lh, lsem.at[0], lsem.at[1], to_mirror)
+    is_early = z == 0
+
+    def send_help():
+        for i in range(rows // 128):
+            at = slice(i * 128, (i + 1) * 128)
+            total = jnp.maximum(l[1, at], 1e-30)
+            oh[at] = (acc[1, at] / total).astype(jnp.bfloat16)
+            log = m[1, at] + jnp.log2(total)
+            lh_out[i:i + 1] = jnp.sum(jnp.where(eye, log, 0.0), axis=0, keepdims=True)
+        log_copy.start()
+        out_copy.start()
+
     def both(half, _):
         first = half == 0
         r0, r1 = 2 * half, 2 * half + 1
@@ -233,57 +263,74 @@
 
         @pl.when(first)
         def _():
+            own_quarter(2, True)
             x2_quarter(0, True)
-        up_quarter(r1, False)
-        x_quarters(r1)
-
-        @pl.when(first)
-        def _():
-            own_quarter(2, True)
-        sib_near(r0)
-        sib_near(r1)
-        single_and_half(half)
-
-        @pl.when(first)
-        def _():
             own_quarter(3, False)
-            up_quarter(2, True)
-            x_quarters(2)
+            up_quarter(1, False)
+
+        sib_own(r0)
+        sib_own(r1)
 
         def one(i, _):
-            @pl.when(i == 1)
-            def _():
-                x2_quarter(r1, False)
-                sib_far(r0)
-                sib_far(r1)
-
-            pair(i, half)
-
-            @pl.when((i == 1) & first)
+            @pl.when(is_late & (i == 0))
+            def _():
+                sib_up(r0)
+                sib_up(r1)
+
+            @pl.when((is_early & (i == 0)) | (is_late & (i == 1)))
+            def _():
+                @pl.when(first)
+                def _():
+                    x_quarters(1)
+                sib_x(r0)
+                sib_x(r1)
+
+            @pl.when(first & (i == 1))
+            def _():
+                up_quarter(2, True)
+                up_quarter(3, False)
+
+            @pl.when(first & (i == 2))
+            def _():
+                x2_quarter(1, False)
+                x_quarters(2)
+
+            @pl.when(jnp.where(is_early & (half == 1), i == 0, i == 2))
+            def _():
+                sib_x2(r0)
+                sib_x2(r1)
+
+            @pl.when(first & (i == 3))
             def _():
                 x2_quarter(2, True)
+                x_quarters(3)
+
+            @pl.when(is_early & (i == 0))
+            def _():
+                single(half)
+
+            @pl.when(is_late | (i > 0))
+            def _():
+                pair(i, half)
+
+            @pl.when(first & (i == 3))
+            def _():
+                x2_quarter(3, False)
+
+            @pl.when(is_early & (half == 1) & (i == 3 - x))
+            def _():
+                send_help()
             return 0
-        lax.fori_loop(0, 3, one, 0)
+        lax.fori_loop(0, 4, one, 0)
         return 0
 
     lax.fori_loop(0, 2, both, 0)
 
-    eye = (lax.broadcasted_iota(jnp.int32, (128, 128), 0) == lax.broadcasted_iota(jnp.int32, (128, 128), 1))
-    out_copy = remote(oh, qh, osem.at[0], osem.at[1], to_mirror)
-    log_copy = remote(lh_out, lh, lsem.at[0], lsem.at[1], to_mirror)
-
-    @pl.when(z == 0)
+    @pl.when(is_early)
     def _():
-        for i in range(rows // 128):
-            at = slice(i * 128, (i + 1) * 128)
-            oh[at] = (acc[1, at] / l[1, at]).astype(jnp.bfloat16)
-            log = m[1, at] + jnp.log2(l[1, at])
-            lh_out[i:i + 1] = jnp.sum(jnp.where(eye, log, 0.0), axis=0, keepdims=True)
-        log_copy.start()
-        out_copy.start()
         o_ref[...] = (acc[0] / l[0]).astype(jnp.bfloat16)
 
-    @pl.when(z == 1)
+    @pl.when(is_late)
     def _():
         query_copy.wait_send()
         log_copy.wait_recv()
@@ -321,9 +368,12 @@
     out = pl.pallas_call(
         kernel,
         out_shape=jax.ShapeDtypeStruct((rows, width), bf16),
-        in_specs=[pl.BlockSpec(memory_space=pltpu.VMEM)] * 3,
+        in_specs=[pl.BlockSpec(memory_space=pltpu.HBM)] * 3,
         out_specs=pl.BlockSpec(memory_space=pltpu.VMEM),
         scratch_shapes=[
+            pltpu.VMEM((rows, width), bf16),
+            pltpu.VMEM(key_states.shape, bf16),
+            pltpu.VMEM(value_states.shape, bf16),
             pltpu.VMEM((BLOCKS, 4, 8, 64, width), bf16),
             pltpu.VMEM((8, 64, width), bf16),
             pltpu.VMEM((256, width), f32),
@@ -342,11 +392,12 @@
             dma((2,)),
             dma((2,)),
             dma((2,)),
+            dma((3,)),
         ],
         name="folded_attention",
         cost_estimate=pl.CostEstimate(flops=4 * 128 * 8 * 1024 * 1024, bytes_accessed=2**20, transcendentals=2**23),
         compiler_params=pltpu.CompilerParams(
-            collective_id=0, has_side_effects=True, vmem_limit_bytes=48 * 2**20),
+            collective_id=0, has_side_effects=True, vmem_limit_bytes=62 * 2**20),
     )(queries.reshape(rows, width), key_states, value_states)
     return out[:, None, :]
 

time: 77.9 us -> 66.9 us (0.86)
  the two profiles are of different devices: /device:TPU:64 before, /device:TPU:1 now
where the time goes in v2:
time: 66.9 us; the launch traced here: 66.8 us
  Pallas kernels  65.1 us (97%)
  local copies, waits for them, and re-layouts  1.67 us (2%)
    pallas_call x1, Pallas kernels, per_device(): pl.pallas_call(kernel, out_shape=jax.ShapeDtypeStruct((rows, width), bf16...  65.1 us
    unnamed x1, local copies, waits for them, and re-layouts  1.67 us

profile of v2, /device:TPU:1, one launch (start us, length us, event | category | flops | bytes accessed | tf_op | source)
XLA Modules:
  0.0 66.8 jit_solution(15456632570977297155)
XLA Ops:
  0.0 65.1 %folded_attention.1 = bf16[1024,128]{1,0:T(8,128)(2,1)} custom-call(bf16[1024,128]{1,0:T(8,128)(2,1)} %bitcast.3, bf16[32,8,128]{2,1,0:T(8,128)(2,1)} %k_hbm.1, bf16[32,8,128]{2,1,0:T(8,128)(2,1)} %v_hbm.1), custom_call_target="tpu_custom_call" | custom-call | flops 4294967296 | bytes 1048576 | tf_op jit(solution)/shard_map/folded_attention/pallas_call | solution.py:368
  65.1 1.7 %copy.5 = bf16[1024,1,128]{2,0,1:T(8,128)(2,1)} copy(bf16[1024,1,128]{2,0,1:T(8,128)(2,1)} %bitcast.2) | data formatting | bytes 524288

commit v3 on v2

--- a/solution.py
+++ b/solution.py
@@ -15,8 +15,8 @@
 XP, XM, X2, SIB, UP, SIB_XP, SIB_XM, SIB_X2, Y_X2, SIB_UP, Y = range(11)
 
 
-def kernel(q_hbm, k_hbm, v_hbm, o_ref, q_ref, k_ref, v_ref, kv, stage, wide, qc, qh, oh, lh, lh_out, m, l, acc,
-           ss, rs, p1s, p1r, qsem, osem, lsem, isem):
+def kernel(q_hbm, k_hbm, v_hbm, o_ref, q_ref, k_ref, v_ref, kv, stage, wide, qc, qh, oh, lh_out,
+           help_o, help_l, m, l, acc, ss, rs, p1s, p1r, qsem, ssem, osem, isem):
     c = lax.axis_index("ctx")
     h = lax.axis_index("head")
     z, x, core = c // 8, (c // 2) % 4, c % 2
@@ -25,7 +25,7 @@
     tiles = rows // QT
 
     def quarter(r):
-        return (lane + r) % 2 + 2 * ((lane // 2 + r // 2) % 2)
+        return (lane + r // 2) % 2 + 2 * ((lane // 2 + r % 2) % 2)
 
     def device(x_, z_, core_, lane_):
         return {"ctx": z_ * 8 + x_ * 2 + core_, "head": group * 4 + lane_}
@@ -35,11 +35,11 @@
     to_sib = device(x, z, 1 - core, lane)
     to_z = device(x, 1 - z, core, lane)
     to_mirror = device(3 - x, 1 - z, 1 - core, lane)
-    to_y = [None] + [device(x, z, core, quarter(r)) for r in (1, 2, 3)]
-    to_group = [None] + [{"ctx": c, "head": ((group + d) % 8) * 4 + lane} for d in range(1, 8)]
+    to_y = device(x, z, core, quarter(2))
+    to_group = [{"ctx": c, "head": ((group + d % 8) % 8) * 4 + quarter(d // 8)} for d in range(16)]
 
     barrier = pltpu.get_barrier_semaphore()
-    partners = to_group[1:] + to_y[1:] + [to_xp, to_xm, to_x2, to_sib, to_z, to_mirror]
+    partners = to_group[1:] + [to_y, to_xp, to_xm, to_x2, to_sib, to_z, to_mirror]
     for partner in partners:
         pl.semaphore_signal(barrier, inc=1, device_id=partner, device_id_type=MESH)
 
@@ -81,15 +81,15 @@
             src_ref=src, dst_ref=dst, send_sem=send, recv_sem=recv, device_id=to, device_id_type=MESH)
 
     def scatter(d):
-        return remote(stage.at[(group + d) % 8], kv.at[c, lane, group], p1s.at[d], p1r.at[d], to_group[d])
-
-    for d in (4, 3, 5, 2, 6, 1, 7):
+        return remote(stage.at[(group + d % 8) % 8], kv.at[c, lane, group], p1s.at[d], p1r.at[d], to_group[d])
+
+    for d in (4, 3, 5, 2, 6, 1, 7, 12, 11, 13, 10, 14, 9, 15, 8):
         scatter(d).start()
     query_copy = remote(q_ref, qh, qsem.at[0], qsem.at[1], to_mirror)
-
-    @pl.when(z == 1)
-    def _():
-        query_copy.start()
+    is_late = z == 1
+    is_early = z == 0
+
+    pl.when(is_late & (x > 0))(query_copy.start)
 
     def piece(kind, r, block, to):
         q = quarter(r)
@@ -101,49 +101,59 @@
     def from_chip(x_):
         return 2 * x_ + 8 * z * (x_ < x).astype(jnp.int32)
 
-    is_late = z == 1
     own_up = 2 * x + core
-    own_goes = {XP: (z == 0) | (x < 3), XM: (z == 0) | (x < 1), X2: (z == 0) | (x < 2)}
+    own_goes = {XP: x < 3, XM: x < 2 - z, X2: x < 3 - z}
+    up_goes = {XP: is_late & (x == 3), XM: is_late & (x > 0), X2: is_late & (x > 1)}
+    has_xp = is_late | (x == 0) | (x == 3)
+    has_xm = is_late | (x > 0)
+    has_x2 = is_late | (x != 1)
+    helps = is_early & (x < 3)
+    helped = is_late & (x > 0)
     targets = {XP: to_xp, XM: to_xm, X2: to_x2}
 
-    def kinds_x(r_even):
-        return (XP, XM, X2) if r_even else (XP, XM)
-
-    def own_quarter(r, r_even, first=False):
+    def kinds_x(direct):
+        return (X2, XP, XM) if direct else (XP, XM)
+
+    def own_quarter(r, direct, first=False):
         if not first:
             landed(r, c)
         @pl.when(z == 0)
         def _():
             piece(UP, r, c, to_z).start()
 
-        for kind in kinds_x(r_even):
+        for kind in kinds_x(direct):
             @pl.when(own_goes[kind])
             def _(kind=kind):
                 piece(kind, r, c, targets[kind]).start()
 
         piece(SIB, r, c, to_sib).start()
 
-    def up_quarter(r, r_even):
+    def up_quarter(r, direct):
         @pl.when(is_late)
         def _():
             landed(r, own_up)
-            for kind in kinds_x(r_even):
-                @pl.when(jnp.logical_not(own_goes[kind]))
+            for kind in kinds_x(direct):
+                @pl.when(up_goes[kind])
                 def _(kind=kind):
                     piece(kind, r, own_up, targets[kind]).start()
             piece(SIB_UP, r, own_up, to_sib).start()
 
     def x_quarters(r):
-        for kind, source in ((SIB_XP, xp), (SIB_XM, xm)):
+        def take(kind, source):
             landed(r, from_chip(source) + core)
             piece(kind, r, from_chip(source) + core, to_sib).start()
 
-    def x2_quarter(r, r_even):
-        block = from_chip(x2) + core
-        landed(r, block)
-        if r_even:
-            piece(Y_X2, r, block, to_y[1]).start()
-        piece(SIB_X2, r, block, to_sib).start()
+        pl.when(has_xp)(lambda: take(SIB_XP, xp))
+        pl.when(has_xm)(lambda: take(SIB_XM, xm))
+
+    def x2_quarter(r, direct):
+        @pl.when(has_x2)
+        def _():
+            block = from_chip(x2) + core
+            landed(r, block)
+            if direct:
+                piece(Y_X2, r, block, to_y).start()
+            piece(SIB_X2, r, block, to_sib).start()
 
     def sib_own(r):
         landed(r, c + 1 - 2 * core)
@@ -152,11 +162,18 @@
         landed(r, own_up + 1 - 2 * core)
 
     def sib_x(r):
-        landed(r, from_chip(xp) + 1 - core)
-        landed(r, from_chip(xm) + 1 - core)
+        @pl.when(has_xp)
+        def _():
+            landed(r, from_chip(xp) + 1 - core)
+
+        @pl.when(has_xm)
+        def _():
+            landed(r, from_chip(xm) + 1 - core)
 
     def sib_x2(r):
-        landed(r, from_chip(x2) + 1 - core)
+        @pl.when(has_x2)
+        def _():
+            landed(r, from_chip(x2) + 1 - core)
 
     def attend(job, parts):
         scores = []
@@ -202,8 +219,8 @@
         attend(0, parts)
 
     def single(half):
-        keys, values = load([jnp.where(core == 0, 6 - 2 * x, 2 * x)], half, 0, 8)
-        attend(1 - core, [(keys, values, None)] * tiles)
+        keys, values = load([2 * x], half, 0, 8)
+        attend(0, [(keys, values, None)] * tiles)
 
     def by_x(a0, a1, a2, a3):
         return jnp.where(x == 0, a0, jnp.where(x == 1, a1, jnp.where(x == 2, a2, a3)))
@@ -225,140 +242,151 @@
         keys, values = load(blocks, half, 0, 8)
         attend(job, [(keys, values, None)] * tiles)
 
-    for d in range(1, 8):
-        scatter(d).wait_recv()
-    for step in (1, 2, 3):
-        piece_y = remote(kv.at[c, lane], kv.at[c, lane], ss.at[Y, step], rs.at[c, lane], to_y[step])
-        piece_y.start()
-    own_quarter(0, True, True)
-
-    @pl.when(z == 0)
-    def _():
-        query_copy.wait_recv()
-        split_scaled(1, qh)
-
-    up_quarter(0, True)
-    x_quarters(0)
-    own_quarter(1, False)
+    def exchange(r):
+        q = quarter(r)
+        return remote(kv.at[c, q], kv.at[c, q], ss.at[Y, r], rs.at[c, q], to_y)
+
+    for r, pieces in ((0, range(1, 8)), (1, range(8, 16))):
+        for d in pieces:
+            scatter(d).wait_recv()
+        exchange(r).start()
+        own_quarter(r, True, True)
 
     eye = (lax.broadcasted_iota(jnp.int32, (128, 128), 0) == lax.broadcasted_iota(jnp.int32, (128, 128), 1))
-    out_copy = remote(oh, qh, osem.at[0], osem.at[1], to_mirror)
-    log_copy = remote(lh_out, lh, lsem.at[0], lsem.at[1], to_mirror)
-    is_early = z == 0
-
-    def send_help():
+    log_copy = remote(lh_out, help_l, ssem.at[0], ssem.at[1], to_mirror)
+    part_copies = [remote(oh.at[pl.ds(i * QT, QT)], help_o.at[pl.ds(i * QT, QT)], osem.at[i], osem.at[tiles + i], to_mirror)
+                   for i in range(tiles)]
+
+    def send_part():
         for i in range(rows // 128):
             at = slice(i * 128, (i + 1) * 128)
-            total = jnp.maximum(l[1, at], 1e-30)
-            oh[at] = (acc[1, at] / total).astype(jnp.bfloat16)
-            log = m[1, at] + jnp.log2(total)
+            log = m[1, at] + jnp.log2(l[1, at])
             lh_out[i:i + 1] = jnp.sum(jnp.where(eye, log, 0.0), axis=0, keepdims=True)
         log_copy.start()
-        out_copy.start()
+        for i, copy in enumerate(part_copies):
+            at = slice(i * QT, (i + 1) * QT)
+            oh[at] = (acc[1, at] / l[1, at]).astype(jnp.bfloat16)
+            copy.start()
 
     def both(half, _):
         first = half == 0
         r0, r1 = 2 * half, 2 * half + 1
-        diagonal(half)
-
-        @pl.when(first)
-        def _():
-            own_quarter(2, True)
-            x2_quarter(0, True)
-            own_quarter(3, False)
-            up_quarter(1, False)
-
-        sib_own(r0)
-        sib_own(r1)
 
         def one(i, _):
-            @pl.when(is_late & (i == 0))
-            def _():
-                sib_up(r0)
-                sib_up(r1)
-
-            @pl.when((is_early & (i == 0)) | (is_late & (i == 1)))
-            def _():
-                @pl.when(first)
+            @pl.when(jnp.where(is_early & (half == 1), i == 4, i == 0))
+            def _():
+                diagonal(half)
+
+            @pl.when(first & (i == 0))
+            def _():
+                own_quarter(2, False)
+                up_quarter(0, True)
+                pl.when(is_early)(lambda: x_quarters(0))
+                own_quarter(3, False)
+                up_quarter(1, True)
+                pl.when(is_early)(lambda: x2_quarter(0, True))
+
+                @pl.when(helps)
                 def _():
-                    x_quarters(1)
+                    query_copy.wait_recv()
+                    split_scaled(1, qh)
+
+            @pl.when(i == 0)
+            def _():
+                sib_own(r0)
+                sib_own(r1)
+
+                @pl.when(is_late)
+                def _():
+                    sib_up(r0)
+                    sib_up(r1)
+
+            @pl.when(first & (i == 1))
+            def _():
+                up_quarter(2, False)
+
+                @pl.when(is_late)
+                def _():
+                    x_quarters(0)
+                    x2_quarter(0, True)
+                x_quarters(1)
+                up_quarter(3, False)
+                x2_quarter(1, True)
+
+            @pl.when(i == 1)
+            def _():
                 sib_x(r0)
                 sib_x(r1)
 
-            @pl.when(first & (i == 1))
-            def _():
-                up_quarter(2, True)
-                up_quarter(3, False)
-
             @pl.when(first & (i == 2))
             def _():
-                x2_quarter(1, False)
                 x_quarters(2)
 
-            @pl.when(jnp.where(is_early & (half == 1), i == 0, i == 2))
+            @pl.when(i == jnp.where(is_late, 3, jnp.where(first, 2, 1)))
             def _():
                 sib_x2(r0)
                 sib_x2(r1)
 
             @pl.when(first & (i == 3))
             def _():
-                x2_quarter(2, True)
+                x2_quarter(2, False)
                 x_quarters(3)
 
-            @pl.when(is_early & (i == 0))
+            @pl.when((core == 1) & (i == 0))
             def _():
                 single(half)
 
-            @pl.when(is_late | (i > 0))
+            @pl.when((i < 4) & (is_late | (i > 0)))
             def _():
                 pair(i, half)
 
-            @pl.when(first & (i == 3))
-            def _():
-                x2_quarter(3, False)
-
-            @pl.when(is_early & (half == 1) & (i == 3 - x))
-            def _():
-                send_help()
+            @pl.when(helps & (half == 1) & (i == 3 - x))
+            def _():
+                send_part()
             return 0
-        lax.fori_loop(0, 4, one, 0)
+        lax.fori_loop(0, 5, one, 0)
+        pl.when(first)(lambda: x2_quarter(3, False))
         return 0
 
     lax.fori_loop(0, 2, both, 0)
 
-    @pl.when(is_early)
+    @pl.when(jnp.logical_not(helped))
     def _():
         o_ref[...] = (acc[0] / l[0]).astype(jnp.bfloat16)
 
-    @pl.when(is_late)
+    @pl.when(helped)
     def _():
-        query_copy.wait_send()
         log_copy.wait_recv()
-        out_copy.wait_recv()
         for i in range(rows // 128):
+            if i % (QT // 128) == 0:
+                part_copies[i * 128 // QT].wait_recv()
             at = slice(i * 128, (i + 1) * 128)
-            log = jnp.sum(jnp.where(eye, lh[i:i + 1], 0.0), axis=1, keepdims=True)
+            log = jnp.sum(jnp.where(eye, help_l[i:i + 1], 0.0), axis=1, keepdims=True)
             mine = m[0, at]
             top = jnp.maximum(mine, log)
             w_mine, w_help = jnp.exp2(mine - top), jnp.exp2(log - top)
             total = l[0, at] * w_mine + w_help
-            mixed = acc[0, at] * w_mine + qh[at].astype(jnp.float32) * w_help
+            mixed = acc[0, at] * w_mine + help_o[at].astype(jnp.float32) * w_help
             o_ref[at] = (mixed / total).astype(jnp.bfloat16)
-
-    @pl.when(z == 0)
+        query_copy.wait_send()
+
+    @pl.when(helps)
     def _():
-        log_copy.wait_send()
-        out_copy.wait_send()
-    for d in range(1, 8):
+        for copy in [log_copy] + part_copies:
+            copy.wait_send()
+    for d in range(1, 16):
         scatter(d).wait_send()
     for r in range(4):
-        kinds = [XP, XM, SIB, SIB_XP, SIB_XM, SIB_X2] + ([X2, Y_X2] if r % 2 == 0 else []) + ([Y] if r else [])
-        for kind in kinds:
-            piece(kind, r, c, to_sib).wait_send()
-        for kind, when in ((UP, z == 0), (SIB_UP, z == 1)):
-            @pl.when(when)
-            def _(kind=kind):
-                piece(kind, r, c, to_sib).wait_send()
+        sent = [(XP, own_goes[XP] | up_goes[XP]), (XM, own_goes[XM] | up_goes[XM]), (SIB, None), (SIB_XP, has_xp),
+                (SIB_XM, has_xm), (SIB_X2, has_x2), (UP, is_early), (SIB_UP, is_late)]
+        if r < 2:
+            sent += [(X2, own_goes[X2] | up_goes[X2]), (Y_X2, has_x2), (Y, None)]
+        for kind, when in sent:
+            wait = piece(kind, r, c, to_sib).wait_send
+            if when is None:
+                wait()
+            else:
+                pl.when(when)(wait)
 
 
 def per_device(queries, key_states, value_states):
@@ -381,17 +409,18 @@
             pltpu.VMEM((rows, width), bf16),
             pltpu.VMEM((rows, width), bf16),
             pltpu.VMEM((8, 128), f32),
+            pltpu.VMEM((rows, width), bf16),
             pltpu.VMEM((8, 128), f32),
             pltpu.VMEM((2, rows, width), f32),
             pltpu.VMEM((2, rows, width), f32),
             pltpu.VMEM((2, rows, width), f32),
             dma((11, 4)),
             dma((BLOCKS, 4)),
-            dma((8,)),
-            dma((8,)),
+            dma((16,)),
+            dma((16,)),
             dma((2,)),
             dma((2,)),
-            dma((2,)),
+            dma((8,)),
             dma((3,)),
         ],
         name="folded_attention",

time: 66.9 us -> 61.2 us (0.915)
  the two profiles are of different devices: /device:TPU:1 before, /device:TPU:67 now
where the time goes in v3:
time: 61.2 us; the launch traced here: 61 us
  Pallas kernels  59.4 us (97%)
  local copies, waits for them, and re-layouts  1.67 us (3%)
    pallas_call x1, Pallas kernels, per_device(): pl.pallas_call(kernel, out_shape=jax.ShapeDtypeStruct((rows, width), bf16...  59.4 us
    unnamed x1, local copies, waits for them, and re-layouts  1.67 us

profile of v3, /device:TPU:67, one launch (start us, length us, event | category | flops | bytes accessed | tf_op | source)
XLA Modules:
  0.0 61.0 jit_solution(9724582284867828429)
XLA Ops:
  0.0 59.4 %folded_attention.1 = bf16[1024,128]{1,0:T(8,128)(2,1)} custom-call(bf16[1024,128]{1,0:T(8,128)(2,1)} %bitcast.3, bf16[32,8,128]{2,1,0:T(8,128)(2,1)} %k_hbm.1, bf16[32,8,128]{2,1,0:T(8,128)(2,1)} %v_hbm.1), custom_call_target="tpu_custom_call" | custom-call | flops 4294967296 | bytes 1048576 | tf_op jit(solution)/shard_map/folded_attention/pallas_call | solution.py:396
  59.4 1.7 %copy.5 = bf16[1024,1,128]{2,0,1:T(8,128)(2,1)} copy(bf16[1024,1,128]{2,0,1:T(8,128)(2,1)} %bitcast.2) | data formatting | bytes 524288

commit v4 on v3

--- a/solution.py
+++ b/solution.py
@@ -291,6 +291,12 @@
                     query_copy.wait_recv()
                     split_scaled(1, qh)
 
+            @pl.when((half == 1) & (i == 0))
+            def _():
+                x2_quarter(2, False)
+                x_quarters(3)
+                x2_quarter(3, False)
+
             @pl.when(i == 0)
             def _():
                 sib_own(r0)
@@ -313,7 +319,7 @@
                 up_quarter(3, False)
                 x2_quarter(1, True)
 
-            @pl.when(i == 1)
+            @pl.when(i == jnp.where(is_early & (x < 2), 2, 1))
             def _():
                 sib_x(r0)
                 sib_x(r1)
@@ -322,17 +328,12 @@
             def _():
                 x_quarters(2)
 
-            @pl.when(i == jnp.where(is_late, 3, jnp.where(first, 2, 1)))
+            @pl.when(i == jnp.where(is_late | (x != 2), 3, jnp.where(first, 2, 1)))
             def _():
                 sib_x2(r0)
                 sib_x2(r1)
 
-            @pl.when(first & (i == 3))
-            def _():
-                x2_quarter(2, False)
-                x_quarters(3)
-
-            @pl.when((core == 1) & (i == 0))
+            @pl.when((core == 1) & (i == jnp.where(is_early & (half == 1), 4, 0)))
             def _():
                 single(half)
 
@@ -345,7 +346,6 @@
                 send_part()
             return 0
         lax.fori_loop(0, 5, one, 0)
-        pl.when(first)(lambda: x2_quarter(3, False))
         return 0
 
     lax.fori_loop(0, 2, both, 0)

time: 61.2 us -> 60.6 us (level)
  no operation moved by 1% of the time
where the time goes in v4:
time: 60.6 us; the launch traced here: 60.4 us
  Pallas kernels  58.8 us (97%)
  local copies, waits for them, and re-layouts  1.67 us (3%)
    pallas_call x1, Pallas kernels, per_device(): pl.pallas_call(kernel, out_shape=jax.ShapeDtypeStruct((rows, width), bf16...  58.8 us
    unnamed x1, local copies, waits for them, and re-layouts  1.67 us

profile of v4, /device:TPU:67, one launch (start us, length us, event | category | flops | bytes accessed | tf_op | source)
XLA Modules:
  0.0 60.4 jit_solution(208821549196295190)
XLA Ops:
  0.0 58.8 %folded_attention.1 = bf16[1024,128]{1,0:T(8,128)(2,1)} custom-call(bf16[1024,128]{1,0:T(8,128)(2,1)} %bitcast.3, bf16[32,8,128]{2,1,0:T(8,128)(2,1)} %k_hbm.1, bf16[32,8,128]{2,1,0:T(8,128)(2,1)} %v_hbm.1), custom_call_target="tpu_custom_call" | custom-call | flops 4294967296 | bytes 1048576 | tf_op jit(solution)/shard_map/folded_attention/pallas_call | solution.py:396
  58.8 1.7 %copy.5 = bf16[1024,1,128]{2,0,1:T(8,128)(2,1)} copy(bf16[1024,1,128]{2,0,1:T(8,128)(2,1)} %bitcast.2) | data formatting | bytes 524288

commit v5 on v4

--- a/solution.py
+++ b/solution.py
@@ -112,7 +112,7 @@
     targets = {XP: to_xp, XM: to_xm, X2: to_x2}
 
     def kinds_x(direct):
-        return (X2, XP, XM) if direct else (XP, XM)
+        return (XP, XM, X2) if direct else (XP, XM)
 
     def own_quarter(r, direct, first=False):
         if not first:

time: 60.6 us -> 60.6 us (level)
  no operation moved by 1% of the time
where the time goes in v5:
time: 60.6 us; the launch traced here: 60.4 us
  Pallas kernels  58.8 us (97%)
  local copies, waits for them, and re-layouts  1.67 us (3%)
    pallas_call x1, Pallas kernels, per_device(): pl.pallas_call(kernel, out_shape=jax.ShapeDtypeStruct((rows, width), bf16...  58.8 us
    unnamed x1, local copies, waits for them, and re-layouts  1.67 us

profile of v5, /device:TPU:67, one launch (start us, length us, event | category | flops | bytes accessed | tf_op | source)
XLA Modules:
  0.0 60.4 jit_solution(14014726887408564438)
XLA Ops:
  0.0 58.8 %folded_attention.1 = bf16[1024,128]{1,0:T(8,128)(2,1)} custom-call(bf16[1024,128]{1,0:T(8,128)(2,1)} %bitcast.3, bf16[32,8,128]{2,1,0:T(8,128)(2,1)} %k_hbm.1, bf16[32,8,128]{2,1,0:T(8,128)(2,1)} %v_hbm.1), custom_call_target="tpu_custom_call" | custom-call | flops 4294967296 | bytes 1048576 | tf_op jit(solution)/shard_map/folded_attention/pallas_call | solution.py:396
  58.8 1.7 %copy.5 = bf16[1024,1,128]{2,0,1:T(8,128)(2,1)} copy(bf16[1024,1,128]{2,0,1:T(8,128)(2,1)} %bitcast.2) | data formatting | bytes 524288
